TPU v7x, 32 devices: a whole 2x2x4 slice. The times are simulated.
32 devices in a mesh: dp: 8 (over y, x, core), mp: 4 (over z).
Axes of the slice: x: 2, y: 2, z: 4, core: 2. Of those that a mesh axis runs over, the one named last changes fastest.
Arguments:
- inputs: bfloat16 [8192, 768], P(('dp', 'mp')), may hold values from -6 to 6
- cotangent: bfloat16 [8192, 768], P(('dp', 'mp')), may hold values from -6 to 6
- doc_lengths: int32 [8, 4], P('dp'), may hold values from 1 to 832, as said below
- first_gain: float32 [768], replicated, may hold values from 0.1 to 1.9
- first_shift: float32 [768], replicated, may hold values from -1.5 to 1.5
- qkv_weight: bfloat16 [768, 3, 768], P('dp', None, 'mp'), may hold values from -0.21875 to 0.21875
- qv_bias: float32 [2, 768], P(None, 'mp'), may hold values from -1.5 to 1.5
- out_weight: bfloat16 [768, 768], P('mp', 'dp'), may hold values from -1.75 to 1.75
- out_bias: float32 [768], replicated, may hold values from -1.5 to 1.5
- second_gain: float32 [768], replicated, may hold values from 0.1 to 1.9
- second_shift: float32 [768], replicated, may hold values from -1.5 to 1.5
- up_weight: bfloat16 [768, 3072], P('dp', 'mp'), may hold values from -0.21875 to 0.21875
- up_bias: float32 [3072], P('mp'), may hold values from -1.5 to 1.5
- down_weight: bfloat16 [3072, 768], P('mp', 'dp'), may hold values from -0.109375 to 0.109375
- down_bias: float32 [768], replicated, may hold values from -1.5 to 1.5
Outputs:
- outputs: bfloat16 [8192, 768], P(('dp', 'mp'))
- grad_inputs: bfloat16 [8192, 768], P(('dp', 'mp'))
- grad_first_gain: float32 [768], replicated
- grad_first_shift: float32 [768], replicated
- grad_qkv_weight: float32 [768, 3, 768], P('dp', None, 'mp')
- grad_qv_bias: float32 [2, 768], P(None, 'mp')
- grad_out_weight: float32 [768, 768], P('mp', 'dp')
- grad_out_bias: float32 [768], replicated
- grad_second_gain: float32 [768], replicated
- grad_second_shift: float32 [768], replicated
- grad_up_weight: float32 [768, 3072], P('dp', 'mp')
- grad_up_bias: float32 [3072], P('mp')
- grad_down_weight: float32 [3072, 768], P('mp', 'dp')
- grad_down_bias: float32 [768], replicated
Inputs may be any that keep to these rules, and one draw needn't show every extreme that they name: `doc_lengths`: in each block one document, at a place drawn from the seed, has exactly 832 tokens and the others 1 to 64; the lengths of a block sum to at most 1024, and the rest of the block is padding.
All inputs are finite; a program needn't handle non-finite values.
Results may differ from a plain program's by a relative error of at most 0.012.
The roundings to bfloat16 on the way count: a program that leaves them out, or rounds other values in their place, can miss the bound.
Values may be sent and summed in bfloat16 or wider, within the bound.
A program may use at most 128 MiB of HBM per device.

v0:
```python
import jax
import jax.numpy as jnp
from jax import lax
from jax.sharding import PartitionSpec as P

HEAD_DIM = 64


EPSILON = 1e-05


def layer_norm(values, gain, shift):
    center = values - jnp.mean(values, axis=-1, keepdims=True)
    spread = jnp.mean(center * center, axis=-1, keepdims=True)
    return center * lax.rsqrt(spread + EPSILON) * gain + shift


def smooth_gate(values):
    return jax.nn.gelu(values, approximate=True)


def swap(values, axis, mask):
    count = lax.axis_size(axis)
    return lax.ppermute(values, axis, [(i, i ^ mask) for i in range(count)])


def bits_of(axis):
    return [1 << k for k in range(lax.axis_size(axis).bit_length() - 1)]


def orders(axis):
    bits = bits_of(axis)
    return bits[1:] + bits[:1], bits[:0:-1] + bits[:1]


def gather_blocks(block, axis, order):
    me = lax.axis_index(axis)
    held = block[None]
    for bit in order:
        held = jnp.concatenate([held, swap(held, axis, bit)], axis=0)
    parts = []
    for j in range(lax.axis_size(axis)):
        relative = me ^ j
        slot = sum(((relative // bit) % 2) * (1 << k) for k, bit in enumerate(order))
        parts.append(lax.dynamic_index_in_dim(held, slot, 0, keepdims=False))
    return jnp.concatenate(parts, axis=0)


def first_half(left, right, axis, order):
    me = lax.axis_index(axis)
    bits = bits_of(axis)[::-1]
    rows = left.shape[1] // lax.axis_size(axis)
    split = left.reshape(left.shape[:1] + (2,) * len(bits) + (rows,))
    side = (me // order[-1]) % 2
    sent, kept = (
        dot_rows(
            lax.dynamic_index_in_dim(
                split, half, 1 + bits.index(order[-1]), keepdims=False
            ).reshape(left.shape[0], left.shape[1] // 2),
            right,
        )
        for half in (1 - side, side)
    )
    return sent.astype(jnp.bfloat16), kept


def halve(total, axis, order, step):
    me = lax.axis_index(axis)
    done = order[::-1][:step]
    bits = [bit for bit in bits_of(axis)[::-1] if bit not in done]
    bit = order[::-1][step]
    rows = total.shape[0] // (1 << len(bits))
    total = total.reshape((2,) * len(bits) + (rows,) + total.shape[1:])
    place, side = bits.index(bit), (me // bit) % 2
    sent, kept = (
        lax.dynamic_index_in_dim(total, half, place, keepdims=False).reshape(
            (rows << (len(bits) - 1),) + total.shape[len(bits) + 1 :]
        )
        for half in (1 - side, side)
    )
    return sent.astype(jnp.bfloat16), kept


def meet(halves, axis, order, step):
    sent, kept = halves
    return kept + swap(sent, axis, order[::-1][step]).astype(f32)


def scatter_product(left, right, axis, order):
    total = meet(first_half(left, right, axis, order), axis, order, 0)
    for step in range(1, len(order)):
        total = meet(halve(total, axis, order, step), axis, order, step)
    return total


def gather_chunks(chunk):
    return [chunk] + [swap(chunk, "mp", r) for r in range(1, lax.axis_size("mp"))]


def scatter_chunks(product):
    count = lax.axis_size("mp")
    arrived = [swap(product(r).astype(jnp.bfloat16), "mp", r) for r in range(count - 1, 0, -1)]
    total = product(0)
    for piece in arrived:
        total = total + piece.astype(jnp.float32)
    return total


def sum_over(values, axis):
    bits = bits_of(axis)
    while bits:
        first, bits = bits[:2], bits[2:]
        if len(first) == 2:
            low, high = first
            near, far, both = (swap(values, axis, mask) for mask in (low, high, low ^ high))
            values = (values + near) + (far + both)
        else:
            values = values + swap(values, axis, first[0])
    return values


def after(values, *earlier):
    return lax.optimization_barrier((values, *earlier))[0]


def join(chunks):
    return jnp.concatenate(chunks, axis=0)


def attend_forward(queries, keys, values, segment, places, width, between):
    length, heads_here, head_size = queries.shape
    contexts, logsums = [], []
    for first in range(0, length, width):
        part = slice(first, first + width)
        allowed = (segment[part, None] == segment[None, :]) & (places[part, None] >= places[None, :])
        scores = jnp.einsum(
            "qhe,khe->hqk", queries[part], keys, preferred_element_type=jnp.float32
        )
        scores = jnp.where(allowed[None], scores, -1e30)
        largest = jnp.max(scores, axis=-1, keepdims=True)
        exponent = jnp.exp(scores - largest)
        total = jnp.sum(exponent, axis=-1, keepdims=True)
        weights = (exponent / total).astype(jnp.bfloat16)
        context = jnp.einsum("hqk,khe->qhe", weights, values, preferred_element_type=jnp.float32)
        contexts.append(context.astype(jnp.bfloat16).reshape(width, heads_here * head_size))
        logsums.append(largest + jnp.log(total))
        if first == 0:
            between(contexts[0])
    return join(contexts), logsums


def attend_backward(
    queries, keys, values, grad_context, logsums, segment, places, width, between
):
    length, heads_here, head_size = queries.shape
    grad_keys = jnp.zeros(keys.shape, jnp.float32)
    grad_values = jnp.zeros(keys.shape, jnp.float32)
    grad_queries = []
    for index, first in enumerate(range(0, length, width)):
        part = slice(first, first + width)
        allowed = (segment[part, None] == segment[None, :]) & (places[part, None] >= places[None, :])
        query_block, grad_block = queries[part], grad_context[part]
        scores = jnp.einsum("qhe,khe->hqk", query_block, keys, preferred_element_type=jnp.float32)
        scores = jnp.where(allowed[None], scores, -1e30)
        softmax_weights = jnp.exp(scores - logsums[index])
        grad_values = grad_values + jnp.einsum(
            "hqk,qhe->khe",
            softmax_weights.astype(jnp.bfloat16),
            grad_block,
            preferred_element_type=jnp.float32,
        )
        grad_weights = jnp.einsum(
            "qhe,khe->hqk", grad_block, values, preferred_element_type=jnp.float32
        )
        inner = jnp.sum(softmax_weights * grad_weights, axis=-1, keepdims=True)
        grad_scores = (softmax_weights * (grad_weights - inner)).astype(jnp.bfloat16)
        grad_query = jnp.einsum(
            "hqk,khe->qhe", grad_scores, keys, preferred_element_type=jnp.float32
        )
        grad_keys = grad_keys + jnp.einsum(
            "hqk,qhe->khe", grad_scores, query_block, preferred_element_type=jnp.float32
        )
        grad_queries.append(grad_query.astype(jnp.bfloat16).reshape(width, heads_here * head_size))
        if first == 0:
            between(grad_queries[0])
    return (
        join(grad_queries),
        grad_keys.astype(jnp.bfloat16).reshape(length, heads_here * head_size),
        grad_values.astype(jnp.bfloat16).reshape(length, heads_here * head_size),
    )


ROWS_DIM = (((0,), (0,)), ((), ()))
COLS_DIM = (((1,), (1,)), ((), ()))
f32 = jnp.float32


def dot(left, right):
    return jnp.dot(left, right, preferred_element_type=f32)


def dot_cols(left, right):
    return lax.dot_general(left, right, COLS_DIM, preferred_element_type=f32)


def dot_rows(left, right):
    return lax.dot_general(left, right, ROWS_DIM, preferred_element_type=f32)


def local(
    inputs,
    cotangent,
    doc_lengths,
    first_gain,
    first_shift,
    qkv_weight,
    qv_bias,
    out_weight,
    out_bias,
    second_gain,
    second_shift,
    up_weight,
    up_bias,
    down_weight,
    down_bias,
):
    rows_here = inputs.shape[0]
    group = lax.axis_size("mp")
    length = rows_here * group
    width = min(512, length)
    cols_here = qkv_weight.shape[2]
    heads_here = cols_here // HEAD_DIM
    factor = HEAD_DIM ** (-0.5)
    me = lax.axis_index("mp")
    order_a, order_b = orders("dp")
    ends = jnp.cumsum(doc_lengths[0])
    steps = jnp.arange(rows_here, dtype=jnp.int32)
    places = join([(me ^ r) * rows_here + steps for r in range(group)])
    segment = jnp.sum((places[:, None] >= ends[None, :]).astype(jnp.int32), axis=1)
    valid = (places[:rows_here] < ends[-1]).astype(f32)

    start_values = inputs.astype(f32)
    normed_one = layer_norm(start_values, first_gain, first_shift).astype(jnp.bfloat16)
    chunks_one = gather_chunks(normed_one)
    shard = qkv_weight.reshape(qkv_weight.shape[0], 3 * cols_here)
    whole = gather_blocks(jnp.concatenate([shard, out_weight.T], axis=1), "dp", order_a)
    whole_qkv, whole_out = whole[:, : 3 * cols_here], whole[:, 3 * cols_here :]

    mixed = [dot(chunk, whole_qkv) for chunk in chunks_one]
    queries = join(
        [((m[:, :cols_here] + qv_bias[0]) * factor).astype(jnp.bfloat16) for m in mixed]
    ).reshape(length, heads_here, HEAD_DIM)
    keys_all = join([m[:, cols_here : 2 * cols_here].astype(jnp.bfloat16) for m in mixed]).reshape(
        length, heads_here, HEAD_DIM
    )
    values_all = join(
        [(m[:, 2 * cols_here :] + qv_bias[1]).astype(jnp.bfloat16) for m in mixed]
    ).reshape(length, heads_here, HEAD_DIM)

    hidden_units = up_weight.shape[1] * group
    half = hidden_units // 2

    def halves(values):
        return values[..., :half], values[..., half:]

    late_up, late_bias, late_down, queries, keys_all, values_all = lax.optimization_barrier(
        (up_weight, up_bias, down_weight.T, queries, keys_all, values_all)
    )
    up_chunks = gather_chunks(late_up)
    bias_parts = gather_chunks(late_bias)
    stages = {}

    def midway(block):
        *up, arrived = lax.optimization_barrier((*up_chunks, block))
        stages["up"] = [
            gather_blocks(part, "dp", order)
            for part, order in zip(halves(jnp.concatenate(up, axis=1)), (order_a, order_b))
        ]
        stages["down"] = gather_chunks(after(late_down, *up[1:], block))

    context, logsum = attend_forward(
        queries, keys_all, values_all, segment, places, width, midway
    )
    bias_chunks = jnp.concatenate(list(lax.optimization_barrier((*bias_parts, context)))[:-1])
    whole_up = stages["up"]
    down_chunks = lax.optimization_barrier((*stages["down"], context))[:-1]
    whole_down = [
        gather_blocks(part, "dp", order)
        for part, order in zip(halves(jnp.concatenate(down_chunks, axis=1)), (order_a, order_b))
    ]

    grad_out = cotangent.astype(f32) * valid[:, None]
    grad_out_low = grad_out.astype(jnp.bfloat16)

    def rows_of(values, r):
        return values[r * rows_here : (r + 1) * rows_here]

    hidden = (
        start_values
        + scatter_chunks(lambda r: dot_cols(rows_of(context, r), whole_out))
        + out_bias
    )
    normed_two = layer_norm(hidden, second_gain, second_shift).astype(jnp.bfloat16)
    active, grad_upper = [], []
    for up_part, down_part, bias in zip(whole_up, whole_down, halves(bias_chunks)):
        upper = dot(normed_two, up_part) + bias
        gate_value, gate_pull = jax.vjp(smooth_gate, upper)
        active.append(gate_value.astype(jnp.bfloat16))
        grad_active = dot(grad_out_low, down_part)
        grad_upper.append(gate_pull(grad_active)[0].astype(jnp.bfloat16))
    grad_normed_two = dot_cols(grad_upper[0], whole_up[0]) + dot_cols(grad_upper[1], whole_up[1])
    fed = dot_cols(active[0], whole_down[0]) + dot_cols(active[1], whole_down[1])
    result = (hidden + fed + down_bias).astype(jnp.bfloat16)

    norm_value, second_pull = jax.vjp(layer_norm, hidden, second_gain, second_shift)
    grad_hidden_norm, grad_second_gain, grad_second_shift = second_pull(grad_normed_two)
    grad_hidden = grad_out + grad_hidden_norm
    chunks_hidden = gather_chunks(grad_hidden.astype(jnp.bfloat16))
    grad_context = join([dot(chunk, whole_out).astype(jnp.bfloat16) for chunk in chunks_hidden])

    both = (order_a, order_b) * 2
    firsts = [
        first_half(left, right, "dp", order)
        for (left, right), order in zip(
            [(normed_two, right) for right in grad_upper]
            + [(grad_out_low, right) for right in active],
            both,
        )
    ]
    firsts, grad_context = lax.optimization_barrier((firsts, grad_context))
    sums = [meet(pair, "dp", order, 0) for pair, order in zip(firsts, both)]
    out_sum = scatter_product(join(chunks_hidden), context, "dp", order_b)

    def step_sums(step, value):
        sums[:] = lax.optimization_barrier((sums, value))[0]
        if step < len(order_a):
            sums[:] = [
                meet(halve(total, "dp", order, step), "dp", order, step)
                for total, order in zip(sums, both)
            ]

    bias_sums = jnp.concatenate([jnp.sum(part, axis=0, dtype=f32) for part in grad_upper])
    bias_sums = bias_sums.reshape(group, hidden_units // group)
    grad_up_bias = bias_sums[0]
    for r in range(1, group):
        grad_up_bias = grad_up_bias + swap(bias_sums[r], "mp", r)

    early = jnp.concatenate(
        [
            grad_second_gain,
            grad_second_shift,
            jnp.sum(grad_hidden, axis=0),
            jnp.sum(grad_out, axis=0),
        ]
    )
    model = first_gain.shape[0]
    early = sum_over(jnp.concatenate([sum_over(early, "mp"), grad_up_bias]), "dp")

    grad_queries, grad_keys, grad_values = attend_backward(
        queries,
        keys_all,
        values_all,
        grad_context.reshape(length, heads_here, HEAD_DIM),
        logsum,
        segment,
        places,
        width,
        lambda block: step_sums(1, block),
    )
    grad_queries = grad_queries * factor
    grad_mixed = jnp.concatenate([grad_queries, grad_keys, grad_values], axis=1)
    for step in range(2, len(order_a)):
        step_sums(step, grad_mixed)
    grad_normed_one = scatter_chunks(lambda r: dot_cols(rows_of(grad_mixed, r), whole_qkv))
    step_sums(len(order_a), grad_normed_one)
    size = hidden_units // group

    def own_shard(parts):
        both_halves = jnp.concatenate(parts, axis=1)
        return scatter_chunks(lambda r: both_halves[:, r * size : (r + 1) * size])

    shard_up, shard_down, shard_out = own_shard(sums[:2]), own_shard(sums[2:]).T, out_sum.T
    shard_qkv = scatter_product(join(chunks_one), grad_mixed, "dp", order_a)
    shard_qkv = shard_qkv.reshape(qkv_weight.shape)
    grad_qv_bias = jnp.concatenate(
        [jnp.sum(grad_queries, axis=0, dtype=f32), jnp.sum(grad_values, axis=0, dtype=f32)]
    )
    first_value, first_pull = jax.vjp(layer_norm, start_values, first_gain, first_shift)
    grad_start_norm, grad_first_gain, grad_first_shift = first_pull(grad_normed_one)
    grad_inputs = (grad_hidden + grad_start_norm).astype(jnp.bfloat16)
    late = sum_over(jnp.concatenate([grad_first_gain, grad_first_shift]), "mp")
    late = sum_over(jnp.concatenate([late, grad_qv_bias]), "dp")
    return (
        result,
        grad_inputs,
        late[:model],
        late[model : 2 * model],
        shard_qkv,
        late[2 * model :].reshape(2, cols_here),
        shard_out,
        early[2 * model : 3 * model],
        early[:model],
        early[model : 2 * model],
        shard_up,
        early[4 * model :],
        shard_down,
        early[3 * model : 4 * model],
    )


def solution(mesh):
    placed = (
        P(("dp", "mp"), None),
        P(("dp", "mp"), None),
        P("dp", None),
        P(),
        P(),
        P("dp", None, "mp"),
        P(None, "mp"),
        P("mp", "dp"),
        P(),
        P(),
        P(),
        P("dp", "mp"),
        P("mp"),
        P("mp", "dp"),
        P(),
    )
    return jax.shard_map(
        local,
        mesh=mesh,
        in_specs=placed,
        out_specs=(
            P(("dp", "mp"), None),
            P(("dp", "mp"), None),
            P(),
            P(),
            P("dp", None, "mp"),
            P(None, "mp"),
            P("mp", "dp"),
            P(),
            P(),
            P(),
            P("dp", "mp"),
            P("mp"),
            P("mp", "dp"),
            P(),
        ),
        check_vma=False,
    )
```

profile of v0, /device:TPU:0, one launch (start us, length us, event | category | flops | bytes accessed | tf_op | source)
XLA Modules:
  0.0 420.4 jit_solution(3525790645612304264)
XLA Ops:
  4.4 5.1 %collective-permute-start.5 = (bf16[256,768]{1,0:T(8,128)(2,1)S(1)}, bf16[256,768]{1,0:T(8,128)(2,1)S(1)}, u32[]{:S(2)}, u32[]{:S(2)}) collective-permute-start(bf16[256,768]{1,0:T(8,128)(2,1)S(1)} %fusion.49), channel_id=1, source_target_pairs={{0,3},{1,2},{2,1},{3,0},{4,7},{5,6},{6,5},{7,4},{8,11},{9,10},{10,... | collective-permute-start | bytes 1179656 | tf_op jit(solution)/shard_map/ppermute | solution.py:24
  20.4 8.3 %collective-permute-done.1 = bf16[2,96,768]{1,2,0:T(8,128)(2,1)S(1)} collective-permute-done((bf16[2,96,768]{1,2,0:T(8,128)(2,1)S(1)}, bf16[2,96,768]{1,2,0:T(8,128)(2,1)S(1)}, u32[]{:S(2)}, u32[]{:S(2)}) %collective-permute-start.1) | collective-permute-done | bytes 294944 | tf_op jit(solution)/shard_map/ppermute | solution.py:24
  32.0 11.2 %collective-permute-done.4 = bf16[256,768]{1,0:T(8,128)(2,1)} collective-permute-done((bf16[256,768]{1,0:T(8,128)(2,1)S(1)}, bf16[256,768]{1,0:T(8,128)(2,1)}, u32[]{:S(2)}, u32[]{:S(2)}) %collective-permute-start.4) | collective-permute-done | bytes 393248 | tf_op jit(solution)/shard_map/ppermute | solution.py:24
  43.2 2.4 pad_maximum_fusion.4
  45.5 1.7 copy.63
  56.1 2.5 collective-permute-start.17
  58.6 1.9 collective-permute-start.15
  60.5 2.5 collective-permute-start.11
  66.8 2.0 fusion.44
  72.8 2.4 fusion.45
  77.1 2.0 collective-permute-start.9
  79.1 2.5 collective-permute-start.6
  81.6 4.2 %collective-permute-done.9 = bf16[96,768]{1,0:T(8,128)(2,1)S(1)} collective-permute-done((bf16[96,768]{1,0:T(8,128)(2,1)S(1)}, bf16[96,768]{1,0:T(8,128)(2,1)S(1)}, u32[]{:S(2)}, u32[]{:S(2)}) %collective-permute-start.9) | collective-permute-done | bytes 147488 | tf_op jit(solution)/shard_map/ppermute | solution.py:24
  85.9 2.6 collective-permute-start.20
  88.5 1.8 collective-permute-start.18
  91.0 15.1 %collective-permute-done.20 = bf16[96,768]{1,0:T(8,128)(2,1)S(1)} collective-permute-done((bf16[96,768]{1,0:T(8,128)(2,1)S(1)}, bf16[96,768]{1,0:T(8,128)(2,1)S(1)}, u32[]{:S(2)}, u32[]{:S(2)}) %collective-permute-start.20) | collective-permute-done | bytes 147488 | tf_op jit(solution)/shard_map/ppermute | solution.py:24
  106.1 18.2 %collective-permute-start.8 = (bf16[256,768]{1,0:T(8,128)(2,1)S(1)}, bf16[256,768]{1,0:T(8,128)(2,1)S(1)}, u32[]{:S(2)}, u32[]{:S(2)}) collective-permute-start(bf16[256,768]{1,0:T(8,128)(2,1)S(1)} %convolution_convert_fusion.8), channel_id=1, source_target_pairs={{0,1},{1,0},{2,3},{3,2},{4,5},{5,4},{6,7},{7,6},{8,9},{9,8},{10,11... | collective-permute-start | bytes 1179656 | tf_op jit(solution)/shard_map/ppermute | solution.py:24
  132.7 3.2 collective-permute-done.12
  139.1 1.9 copy.61
  143.0 8.4 %collective-permute-done.13 = bf16[2,96,1536]{2,1,0:T(8,128)(2,1)} collective-permute-done((bf16[2,96,1536]{2,1,0:T(8,128)(2,1)}, bf16[2,96,1536]{2,1,0:T(8,128)(2,1)}, u32[]{:S(2)}, u32[]{:S(2)}) %collective-permute-start.13) | collective-permute-done | bytes 589856 | tf_op jit(solution)/shard_map/ppermute | solution.py:24
  159.0 10.8 %collective-permute-done.28 = bf16[2,96,1536]{2,1,0:T(8,128)(2,1)S(1)} collective-permute-done((bf16[2,96,1536]{2,1,0:T(8,128)(2,1)S(1)}, bf16[2,96,1536]{2,1,0:T(8,128)(2,1)S(1)}, u32[]{:S(2)}, u32[]{:S(2)}) %collective-permute-start.28) | collective-permute-done | bytes 589856 | tf_op jit(solution)/shard_map/ppermute | solution.py:24
  178.5 1.9 convolution_convert_fusion.1
  180.4 1.8 convolution_convert_fusion
  182.2 2.2 fusion.123
  184.4 2.2 fusion.124
  197.3 2.7 collective-permute-start.51
  199.9 1.9 fusion.142
  201.9 1.9 fusion.143
  205.7 2.4 collective-permute-start.54
  208.1 1.8 fusion.39
  211.5 2.5 collective-permute-start.32
  219.4 1.7 collective-permute-start.58
  224.7 23.6 %collective-permute-done.31 = bf16[256,768]{1,0:T(8,128)(2,1)S(1)} collective-permute-done((bf16[256,768]{1,0:T(8,128)(2,1)S(1)}, bf16[256,768]{1,0:T(8,128)(2,1)S(1)}, u32[]{:S(2)}, u32[]{:S(2)}) %collective-permute-start.31) | collective-permute-done | bytes 393248 | tf_op jit(solution)/shard_map/ppermute | solution.py:24
  249.5 2.4 multiply_reduce_fusion.1
  252.0 1.9 multiply_convert_fusion.1
  255.7 1.8 fusion.4
  257.4 2.4 multiply_reduce_fusion
  259.8 1.7 multiply_convert_fusion
  263.4 1.9 convert_reduce_fusion.3
  271.3 2.0 copy.66
  277.5 2.9 collective-permute-start.35
  280.4 3.0 convolution_convert_fusion.4
  287.4 3.5 collective-permute-done.47
  292.6 18.1 %collective-permute-done.34 = bf16[256,768]{1,0:T(8,128)(2,1)} collective-permute-done((bf16[256,768]{1,0:T(8,128)(2,1)}, bf16[256,768]{1,0:T(8,128)(2,1)}, u32[]{:S(2)}, u32[]{:S(2)}) %collective-permute-start.34) | collective-permute-done | bytes 393248 | tf_op jit(solution)/shard_map/ppermute | solution.py:24
  310.7 2.1 fusion.52
  313.4 2.4 collective-permute-start.38
  325.5 3.1 convert_add_fusion.5
  332.9 5.6 %collective-permute-done.44 = bf16[192,576]{1,0:T(8,128)(2,1)S(1)} collective-permute-done((bf16[192,576]{1,0:T(8,128)(2,1)S(1)}, bf16[192,576]{1,0:T(8,128)(2,1)S(1)}, u32[]{:S(2)}, u32[]{:S(2)}) %collective-permute-start.44) | collective-permute-done | bytes 221216 | tf_op jit(solution)/shard_map/ppermute | solution.py:24
  340.5 3.1 collective-permute-done.45
  344.6 1.7 convert_add_fusion.3
  346.6 1.7 convert_add_fusion.2
  348.4 1.8 convert_add_fusion.1
  356.9 11.9 %collective-permute-done.66 = bf16[192,1536]{1,0:T(8,128)(2,1)S(1)} collective-permute-done((bf16[192,1536]{1,0:T(8,128)(2,1)S(1)}, bf16[192,1536]{1,0:T(8,128)(2,1)S(1)}, u32[]{:S(2)}, u32[]{:S(2)}) %collective-permute-start.66) | collective-permute-done | bytes 589856 | tf_op jit(solution)/shard_map/ppermute | solution.py:24
  369.6 9.2 %collective-permute-done.63 = bf16[192,1536]{1,0:T(8,128)(2,1)S(1)} collective-permute-done((bf16[192,1536]{1,0:T(8,128)(2,1)S(1)}, bf16[192,1536]{1,0:T(8,128)(2,1)S(1)}, u32[]{:S(2)}, u32[]{:S(2)}) %collective-permute-start.63) | collective-permute-done | bytes 589856 | tf_op jit(solution)/shard_map/ppermute | solution.py:24
  379.2 1.8 collective-permute-start.69
  383.5 4.8 %collective-permute-done.69 = bf16[96,1536]{1,0:T(8,128)(2,1)S(1)} collective-permute-done((bf16[96,1536]{1,0:T(8,128)(2,1)S(1)}, bf16[96,1536]{1,0:T(8,128)(2,1)S(1)}, u32[]{:S(2)}, u32[]{:S(2)}) %collective-permute-start.69) | collective-permute-done | bytes 294944 | tf_op jit(solution)/shard_map/ppermute | solution.py:24
  388.4 3.1 collective-permute-done.67
  395.4 1.8 collective-permute-start.71
  397.9 2.4 collective-permute-start.74
  400.4 3.0 collective-permute-done.73
  403.3 1.9 collective-permute-start.75
  405.3 2.0 collective-permute-done.71
  407.3 8.4 %collective-permute-done.72 = bf16[96,768]{1,0:T(8,128)(2,1)S(1)} collective-permute-done((bf16[96,768]{1,0:T(8,128)(2,1)S(1)}, bf16[96,768]{1,0:T(8,128)(2,1)S(1)}, u32[]{:S(2)}, u32[]{:S(2)}) %collective-permute-start.72) | collective-permute-done | bytes 147488 | tf_op jit(solution)/shard_map/ppermute | solution.py:24
  416.5 2.7 collective-permute-done.75
  (488 shorter events, 143.0 us)
Async XLA Ops:
  4.4 27.6 %collective-permute-start.5 = (bf16[256,768]{1,0:T(8,128)(2,1)S(1)}, bf16[256,768]{1,0:T(8,128)(2,1)S(1)}, u32[]{:S(2)}, u32[]{:S(2)}) collective-permute-start(bf16[256,768]{1,0:T(8,128)(2,1)S(1)} %fusion.49), channel_id=1, source_target_pairs={{0,3},{1,2},{2,1},{3,0},{4,7},{5,6},{6,5},{7,4},{8,11},{9,10},{10,... | collective-permute-start | bytes 1179656 | tf_op jit(solution)/shard_map/ppermute | solution.py:24
  9.5 33.6 %collective-permute-start.4 = (bf16[256,768]{1,0:T(8,128)(2,1)S(1)}, bf16[256,768]{1,0:T(8,128)(2,1)}, u32[]{:S(2)}, u32[]{:S(2)}) collective-permute-start(bf16[256,768]{1,0:T(8,128)(2,1)S(1)} %fusion.49), channel_id=1, source_target_pairs={{0,2},{1,3},{2,0},{3,1},{4,6},{5,7},{6,4},{7,5},{8,10},{9,11},{10,... | collective-permute-start | bytes 1179656 | tf_op jit(solution)/shard_map/ppermute | solution.py:24
  9.5 33.6 %collective-permute-start.3 = (bf16[256,768]{1,0:T(8,128)(2,1)S(1)}, bf16[256,768]{1,0:T(8,128)(2,1)}, u32[]{:S(2)}, u32[]{:S(2)}) collective-permute-start(bf16[256,768]{1,0:T(8,128)(2,1)S(1)} %fusion.49), channel_id=1, source_target_pairs={{0,1},{1,0},{2,3},{3,2},{4,5},{5,4},{6,7},{7,6},{8,9},{9,8},{10,11... | collective-permute-start | bytes 1179656 | tf_op jit(solution)/shard_map/ppermute | solution.py:24
  12.1 6.5 %collective-permute-start = (bf16[1,96,768]{1,2,0:T(8,128)(2,1)S(1)}, bf16[1,96,768]{1,2,0:T(8,128)(2,1)S(1)}, u32[]{:S(2)}, u32[]{:S(2)}) collective-permute-start(bf16[1,96,768]{1,2,0:T(8,128)(2,1)S(1)} %maximum_bitcast_fusion.4), channel_id=1, source_target_pairs={{0,8},{4,12},{8,0},{12,4},{16,24},{20,28},{24,16},{28,20},{1,9},{5... | collective-permute-start | bytes 442376 | tf_op jit(solution)/shard_map/ppermute | solution.py:24
  18.7 9.9 %collective-permute-start.1 = (bf16[2,96,768]{1,2,0:T(8,128)(2,1)S(1)}, bf16[2,96,768]{1,2,0:T(8,128)(2,1)S(1)}, u32[]{:S(2)}, u32[]{:S(2)}) collective-permute-start(bf16[2,96,768]{1,2,0:T(8,128)(2,1)S(1)} %pad_maximum_fusion.17), channel_id=1, source_target_pairs={{0,16},{4,20},{8,24},{12,28},{16,0},{20,4},{24,8},{28,12},{1,17},{... | collective-permute-start | bytes 884744 | tf_op jit(solution)/shard_map/ppermute | solution.py:24
  29.9 19.9 %collective-permute-start.2 = (bf16[4,96,768]{2,1,0:T(8,128)(2,1)}, bf16[4,96,768]{2,1,0:T(8,128)(2,1)}, u32[]{:S(2)}, u32[]{:S(2)}) collective-permute-start(bf16[4,96,768]{2,1,0:T(8,128)(2,1)} %copy.57), channel_id=1, source_target_pairs={{0,4},{4,0},{8,12},{12,8},{16,20},{20,16},{24,28},{28,24},{1,5},{5... | collective-permute-start | bytes 1769480 | tf_op jit(solution)/shard_map/ppermute | solution.py:24
  56.1 21.0 %collective-permute-start.17 = (f32[768]{0:T(1024)S(1)}, f32[768]{0:T(1024)S(1)}, u32[]{:S(2)}, u32[]{:S(2)}) collective-permute-start(f32[768]{0:T(1024)S(1)} %copy-done.68), channel_id=1, source_target_pairs={{0,3},{1,2},{2,1},{3,0},{4,7},{5,6},{6,5},{7,4},{8,11},{9,10},{10,... | collective-permute-start | bytes 9224 | tf_op jit(solution)/shard_map/ppermute | solution.py:24
  58.6 20.5 %collective-permute-start.16 = (f32[768]{0:T(1024)S(1)}, f32[768]{0:T(1024)S(1)}, u32[]{:S(2)}, u32[]{:S(2)}) collective-permute-start(f32[768]{0:T(1024)S(1)} %copy-done.68), channel_id=1, source_target_pairs={{0,2},{1,3},{2,0},{3,1},{4,6},{5,7},{6,4},{7,5},{8,10},{9,11},{10,... | collective-permute-start | bytes 9224 | tf_op jit(solution)/shard_map/ppermute | solution.py:24
  58.6 23.0 %collective-permute-start.15 = (f32[768]{0:T(1024)S(1)}, f32[768]{0:T(1024)S(1)}, u32[]{:S(2)}, u32[]{:S(2)}) collective-permute-start(f32[768]{0:T(1024)S(1)} %copy-done.68), channel_id=1, source_target_pairs={{0,1},{1,0},{2,3},{3,2},{4,5},{5,4},{6,7},{7,6},{8,9},{9,8},{10,11... | collective-permute-start | bytes 9224 | tf_op jit(solution)/shard_map/ppermute | solution.py:24
  60.5 21.1 %collective-permute-start.11 = (bf16[96,768]{1,0:T(8,128)(2,1)S(1)}, bf16[96,768]{1,0:T(8,128)(2,1)S(1)}, u32[]{:S(2)}, u32[]{:S(2)}) collective-permute-start(bf16[96,768]{1,0:T(8,128)(2,1)S(1)} %copy-done.40), channel_id=1, source_target_pairs={{0,3},{1,2},{2,1},{3,0},{4,7},{5,6},{6,5},{7,4},{8,11},{9,10},{10,... | collective-permute-start | bytes 442376 | tf_op jit(solution)/shard_map/ppermute | solution.py:24
  63.0 18.7 %collective-permute-start.10 = (bf16[96,768]{1,0:T(8,128)(2,1)S(1)}, bf16[96,768]{1,0:T(8,128)(2,1)S(1)}, u32[]{:S(2)}, u32[]{:S(2)}) collective-permute-start(bf16[96,768]{1,0:T(8,128)(2,1)S(1)} %copy-done.40), channel_id=1, source_target_pairs={{0,2},{1,3},{2,0},{3,1},{4,6},{5,7},{6,4},{7,5},{8,10},{9,11},{10,... | collective-permute-start | bytes 442376 | tf_op jit(solution)/shard_map/ppermute | solution.py:24
  77.1 8.8 %collective-permute-start.9 = (bf16[96,768]{1,0:T(8,128)(2,1)S(1)}, bf16[96,768]{1,0:T(8,128)(2,1)S(1)}, u32[]{:S(2)}, u32[]{:S(2)}) collective-permute-start(bf16[96,768]{1,0:T(8,128)(2,1)S(1)} %copy-done.40), channel_id=1, source_target_pairs={{0,1},{1,0},{2,3},{3,2},{4,5},{5,4},{6,7},{7,6},{8,9},{9,8},{10,11... | collective-permute-start | bytes 442376 | tf_op jit(solution)/shard_map/ppermute | solution.py:24
  79.1 50.8 %collective-permute-start.6 = (bf16[256,768]{1,0:T(8,128)(2,1)S(1)}, bf16[256,768]{1,0:T(8,128)(2,1)S(1)}, u32[]{:S(2)}, u32[]{:S(2)}) collective-permute-start(bf16[256,768]{1,0:T(8,128)(2,1)S(1)} %convolution_convert_fusion.10), channel_id=1, source_target_pairs={{0,3},{1,2},{2,1},{3,0},{4,7},{5,6},{6,5},{7,4},{8,11},{9,10},{10,... | collective-permute-start | bytes 1179656 | tf_op jit(solution)/shard_map/ppermute | solution.py:24
  81.6 48.8 %collective-permute-start.7 = (bf16[256,768]{1,0:T(8,128)(2,1)S(1)}, bf16[256,768]{1,0:T(8,128)(2,1)S(1)}, u32[]{:S(2)}, u32[]{:S(2)}) collective-permute-start(bf16[256,768]{1,0:T(8,128)(2,1)S(1)} %convolution_convert_fusion.9), channel_id=1, source_target_pairs={{0,2},{1,3},{2,0},{3,1},{4,6},{5,7},{6,4},{7,5},{8,10},{9,11},{10,... | collective-permute-start | bytes 1179656 | tf_op jit(solution)/shard_map/ppermute | solution.py:24
  85.9 20.2 %collective-permute-start.20 = (bf16[96,768]{1,0:T(8,128)(2,1)S(1)}, bf16[96,768]{1,0:T(8,128)(2,1)S(1)}, u32[]{:S(2)}, u32[]{:S(2)}) collective-permute-start(bf16[96,768]{1,0:T(8,128)(2,1)S(1)} %bitcast.343), channel_id=1, source_target_pairs={{0,3},{1,2},{2,1},{3,0},{4,7},{5,6},{6,5},{7,4},{8,11},{9,10},{10,... | collective-permute-start | bytes 442376 | tf_op jit(solution)/shard_map/ppermute | solution.py:24
  88.5 36.9 %collective-permute-start.19 = (bf16[96,768]{1,0:T(8,128)(2,1)S(1)}, bf16[96,768]{1,0:T(8,128)(2,1)S(1)}, u32[]{:S(2)}, u32[]{:S(2)}) collective-permute-start(bf16[96,768]{1,0:T(8,128)(2,1)S(1)} %bitcast.344), channel_id=1, source_target_pairs={{0,2},{1,3},{2,0},{3,1},{4,6},{5,7},{6,4},{7,5},{8,10},{9,11},{10,... | collective-permute-start | bytes 442376 | tf_op jit(solution)/shard_map/ppermute | solution.py:24
  88.5 38.5 %collective-permute-start.18 = (bf16[96,768]{1,0:T(8,128)(2,1)S(1)}, bf16[96,768]{1,0:T(8,128)(2,1)S(1)}, u32[]{:S(2)}, u32[]{:S(2)}) collective-permute-start(bf16[96,768]{1,0:T(8,128)(2,1)S(1)} %bitcast.345), channel_id=1, source_target_pairs={{0,1},{1,0},{2,3},{3,2},{4,5},{5,4},{6,7},{7,6},{8,9},{9,8},{10,11... | collective-permute-start | bytes 442376 | tf_op jit(solution)/shard_map/ppermute | solution.py:24
  106.1 26.0 %collective-permute-start.8 = (bf16[256,768]{1,0:T(8,128)(2,1)S(1)}, bf16[256,768]{1,0:T(8,128)(2,1)S(1)}, u32[]{:S(2)}, u32[]{:S(2)}) collective-permute-start(bf16[256,768]{1,0:T(8,128)(2,1)S(1)} %convolution_convert_fusion.8), channel_id=1, source_target_pairs={{0,1},{1,0},{2,3},{3,2},{4,5},{5,4},{6,7},{7,6},{8,9},{9,8},{10,11... | collective-permute-start | bytes 1179656 | tf_op jit(solution)/shard_map/ppermute | solution.py:24
  125.4 15.6 %collective-permute-start.24 = (bf16[1,96,1536]{2,1,0:T(8,128)(2,1)}, bf16[1,96,1536]{2,1,0:T(8,128)(2,1)}, u32[]{:S(2)}, u32[]{:S(2)}) collective-permute-start(bf16[1,96,1536]{2,1,0:T(8,128)(2,1)} %maximum_bitcast_fusion.2), channel_id=1, source_target_pairs={{0,16},{4,20},{8,24},{12,28},{16,0},{20,4},{24,8},{28,12},{1,17},{... | collective-permute-start | bytes 884744 | tf_op jit(solution)/shard_map/ppermute | solution.py:24
  126.9 9.0 %collective-permute-start.12 = (bf16[1,96,1536]{2,1,0:T(8,128)(2,1)S(1)}, bf16[1,96,1536]{2,1,0:T(8,128)(2,1)S(1)}, u32[]{:S(2)}, u32[]{:S(2)}) collective-permute-start(bf16[1,96,1536]{2,1,0:T(8,128)(2,1)S(1)} %maximum_bitcast_fusion), channel_id=1, source_target_pairs={{0,8},{4,12},{8,0},{12,4},{16,24},{20,28},{24,16},{28,20},{1,9},{5... | collective-permute-start | bytes 884744 | tf_op jit(solution)/shard_map/ppermute | solution.py:24
  129.9 22.9 %collective-permute-start.27 = (bf16[1,96,1536]{2,1,0:T(8,128)(2,1)}, bf16[1,96,1536]{2,1,0:T(8,128)(2,1)}, u32[]{:S(2)}, u32[]{:S(2)}) collective-permute-start(bf16[1,96,1536]{2,1,0:T(8,128)(2,1)} %maximum_bitcast_fusion.3), channel_id=1, source_target_pairs={{0,16},{4,20},{8,24},{12,28},{16,0},{20,4},{24,8},{28,12},{1,17},{... | collective-permute-start | bytes 884744 | tf_op jit(solution)/shard_map/ppermute | solution.py:24
  130.4 24.5 %collective-permute-start.21 = (bf16[1,96,1536]{2,1,0:T(8,128)(2,1)}, bf16[1,96,1536]{2,1,0:T(8,128)(2,1)}, u32[]{:S(2)}, u32[]{:S(2)}) collective-permute-start(bf16[1,96,1536]{2,1,0:T(8,128)(2,1)} %maximum_bitcast_fusion.1), channel_id=1, source_target_pairs={{0,8},{4,12},{8,0},{12,4},{16,24},{20,28},{24,16},{28,20},{1,9},{5... | collective-permute-start | bytes 884744 | tf_op jit(solution)/shard_map/ppermute | solution.py:24
  136.9 14.5 %collective-permute-start.13 = (bf16[2,96,1536]{2,1,0:T(8,128)(2,1)}, bf16[2,96,1536]{2,1,0:T(8,128)(2,1)}, u32[]{:S(2)}, u32[]{:S(2)}) collective-permute-start(bf16[2,96,1536]{2,1,0:T(8,128)(2,1)} %pad_maximum_fusion.13), channel_id=1, source_target_pairs={{0,16},{4,20},{8,24},{12,28},{16,0},{20,4},{24,8},{28,12},{1,17},{... | collective-permute-start | bytes 1769480 | tf_op jit(solution)/shard_map/ppermute | solution.py:24
  142.1 15.5 %collective-permute-start.25 = (bf16[2,96,1536]{2,1,0:T(8,128)(2,1)S(1)}, bf16[2,96,1536]{2,1,0:T(8,128)(2,1)S(1)}, u32[]{:S(2)}, u32[]{:S(2)}) collective-permute-start(bf16[2,96,1536]{2,1,0:T(8,128)(2,1)S(1)} %pad_maximum_fusion.15), channel_id=1, source_target_pairs={{0,8},{4,12},{8,0},{12,4},{16,24},{20,28},{24,16},{28,20},{1,9},{5... | collective-permute-start | bytes 1769480 | tf_op jit(solution)/shard_map/ppermute | solution.py:24
  152.8 20.0 %collective-permute-start.14 = (bf16[4,96,1536]{2,1,0:T(8,128)(2,1)S(1)}, bf16[4,96,1536]{2,1,0:T(8,128)(2,1)S(1)}, u32[]{:S(2)}, u32[]{:S(2)}) collective-permute-start(bf16[4,96,1536]{2,1,0:T(8,128)(2,1)S(1)} %pad_maximum_fusion.7), channel_id=1, source_target_pairs={{0,4},{4,0},{8,12},{12,8},{16,20},{20,16},{24,28},{28,24},{1,5},{5... | collective-permute-start | bytes 3538952 | tf_op jit(solution)/shard_map/ppermute | solution.py:24
  154.0 15.8 %collective-permute-start.28 = (bf16[2,96,1536]{2,1,0:T(8,128)(2,1)S(1)}, bf16[2,96,1536]{2,1,0:T(8,128)(2,1)S(1)}, u32[]{:S(2)}, u32[]{:S(2)}) collective-permute-start(bf16[2,96,1536]{2,1,0:T(8,128)(2,1)S(1)} %pad_maximum_fusion.16), channel_id=1, source_target_pairs={{0,8},{4,12},{8,0},{12,4},{16,24},{20,28},{24,16},{28,20},{1,9},{5... | collective-permute-start | bytes 1769480 | tf_op jit(solution)/shard_map/ppermute | solution.py:24
  156.1 15.5 %collective-permute-start.22 = (bf16[2,96,1536]{2,1,0:T(8,128)(2,1)S(1)}, bf16[2,96,1536]{2,1,0:T(8,128)(2,1)S(1)}, u32[]{:S(2)}, u32[]{:S(2)}) collective-permute-start(bf16[2,96,1536]{2,1,0:T(8,128)(2,1)S(1)} %pad_maximum_fusion.14), channel_id=1, source_target_pairs={{0,16},{4,20},{8,24},{12,28},{16,0},{20,4},{24,8},{28,12},{1,17},{... | collective-permute-start | bytes 1769480 | tf_op jit(solution)/shard_map/ppermute | solution.py:24
  158.9 17.1 %collective-permute-start.26 = (bf16[4,96,1536]{2,1,0:T(8,128)(2,1)S(1)}, bf16[4,96,1536]{2,1,0:T(8,128)(2,1)S(1)}, u32[]{:S(2)}, u32[]{:S(2)}) collective-permute-start(bf16[4,96,1536]{2,1,0:T(8,128)(2,1)S(1)} %pad_maximum_fusion.9), channel_id=1, source_target_pairs={{0,4},{4,0},{8,12},{12,8},{16,20},{20,16},{24,28},{28,24},{1,5},{5... | collective-permute-start | bytes 3538952 | tf_op jit(solution)/shard_map/ppermute | solution.py:24
  170.9 15.7 %collective-permute-start.29 = (bf16[4,96,1536]{2,1,0:T(8,128)(2,1)S(1)}, bf16[4,96,1536]{2,1,0:T(8,128)(2,1)S(1)}, u32[]{:S(2)}, u32[]{:S(2)}) collective-permute-start(bf16[4,96,1536]{2,1,0:T(8,128)(2,1)S(1)} %pad_maximum_fusion.10), channel_id=1, source_target_pairs={{0,4},{4,0},{8,12},{12,8},{16,20},{20,16},{24,28},{28,24},{1,5},{5... | collective-permute-start | bytes 3538952 | tf_op jit(solution)/shard_map/ppermute | solution.py:24
  172.7 18.3 %collective-permute-start.23 = (bf16[4,96,1536]{2,1,0:T(8,128)(2,1)S(1)}, bf16[4,96,1536]{2,1,0:T(8,128)(2,1)S(1)}, u32[]{:S(2)}, u32[]{:S(2)}) collective-permute-start(bf16[4,96,1536]{2,1,0:T(8,128)(2,1)S(1)} %pad_maximum_fusion.8), channel_id=1, source_target_pairs={{0,4},{4,0},{8,12},{12,8},{16,20},{20,16},{24,28},{28,24},{1,5},{5... | collective-permute-start | bytes 3538952 | tf_op jit(solution)/shard_map/ppermute | solution.py:24
  197.2 16.8 %collective-permute-start.50 = (f32[3072]{0:T(1024)S(1)}, f32[3072]{0:T(1024)S(1)}, u32[]{:S(2)}, u32[]{:S(2)}) collective-permute-start(f32[3072]{0:T(1024)S(1)} %pad_maximum_fusion.24), channel_id=1, source_target_pairs={{0,2},{1,3},{2,0},{3,1},{4,6},{5,7},{6,4},{7,5},{8,10},{9,11},{10,... | collective-permute-start | bytes 36872 | tf_op jit(solution)/shard_map/ppermute | solution.py:24
  197.3 16.7 %collective-permute-start.51 = (f32[3072]{0:T(1024)S(1)}, f32[3072]{0:T(1024)S(1)}, u32[]{:S(2)}, u32[]{:S(2)}) collective-permute-start(f32[3072]{0:T(1024)S(1)} %pad_maximum_fusion.24), channel_id=1, source_target_pairs={{0,3},{1,2},{2,1},{3,0},{4,7},{5,6},{6,5},{7,4},{8,11},{9,10},{10,... | collective-permute-start | bytes 36872 | tf_op jit(solution)/shard_map/ppermute | solution.py:24
  203.7 7.8 %collective-permute-start.52 = (f32[768]{0:T(1024)S(1)}, f32[768]{0:T(1024)S(1)}, u32[]{:S(2)}, u32[]{:S(2)}) collective-permute-start(f32[768]{0:T(1024)S(1)} %slice.312), channel_id=1, source_target_pairs={{0,1},{1,0},{2,3},{3,2},{4,5},{5,4},{6,7},{7,6},{8,9},{9,8},{10,11... | collective-permute-start | bytes 9224 | tf_op jit(solution)/shard_map/ppermute | solution.py:24
  204.5 6.9 %collective-permute-start.53 = (f32[768]{0:T(1024)S(1)}, f32[768]{0:T(1024)S(1)}, u32[]{:S(2)}, u32[]{:S(2)}) collective-permute-start(f32[768]{0:T(1024)S(1)} %get-tuple-element.184), channel_id=1, source_target_pairs={{0,2},{1,3},{2,0},{3,1},{4,6},{5,7},{6,4},{7,5},{8,10},{9,11},{10,... | collective-permute-start | bytes 9224 | tf_op jit(solution)/shard_map/ppermute | solution.py:24
  205.7 8.2 %collective-permute-start.54 = (f32[768]{0:T(1024)S(1)}, f32[768]{0:T(1024)S(1)}, u32[]{:S(2)}, u32[]{:S(2)}) collective-permute-start(f32[768]{0:T(1024)S(1)} %get-tuple-element.185), channel_id=1, source_target_pairs={{0,3},{1,2},{2,1},{3,0},{4,7},{5,6},{6,5},{7,4},{8,11},{9,10},{10,... | collective-permute-start | bytes 9224 | tf_op jit(solution)/shard_map/ppermute | solution.py:24
  211.5 12.7 %collective-permute-start.32 = (bf16[256,768]{1,0:T(8,128)(2,1)S(1)}, bf16[256,768]{1,0:T(8,128)(2,1)S(1)}, u32[]{:S(2)}, u32[]{:S(2)}) collective-permute-start(bf16[256,768]{1,0:T(8,128)(2,1)S(1)} %get-tuple-element.156), channel_id=1, source_target_pairs={{0,3},{1,2},{2,1},{3,0},{4,7},{5,6},{6,5},{7,4},{8,11},{9,10},{10,... | collective-permute-start | bytes 1179656 | tf_op jit(solution)/shard_map/ppermute | solution.py:24
  221.6 26.7 %collective-permute-start.31 = (bf16[256,768]{1,0:T(8,128)(2,1)S(1)}, bf16[256,768]{1,0:T(8,128)(2,1)S(1)}, u32[]{:S(2)}, u32[]{:S(2)}) collective-permute-start(bf16[256,768]{1,0:T(8,128)(2,1)S(1)} %get-tuple-element.156), channel_id=1, source_target_pairs={{0,2},{1,3},{2,0},{3,1},{4,6},{5,7},{6,4},{7,5},{8,10},{9,11},{10,... | collective-permute-start | bytes 1179656 | tf_op jit(solution)/shard_map/ppermute | solution.py:24
  222.7 26.2 %collective-permute-start.30 = (bf16[256,768]{1,0:T(8,128)(2,1)S(1)}, bf16[256,768]{1,0:T(8,128)(2,1)S(1)}, u32[]{:S(2)}, u32[]{:S(2)}) collective-permute-start(bf16[256,768]{1,0:T(8,128)(2,1)S(1)} %get-tuple-element.156), channel_id=1, source_target_pairs={{0,1},{1,0},{2,3},{3,2},{4,5},{5,4},{6,7},{7,6},{8,9},{9,8},{10,11... | collective-permute-start | bytes 1179656 | tf_op jit(solution)/shard_map/ppermute | solution.py:24
  274.8 8.7 %collective-permute-start.46 = (bf16[384,192]{0,1:T(8,128)(2,1)S(1)}, bf16[384,192]{0,1:T(8,128)(2,1)S(1)}, u32[]{:S(2)}, u32[]{:S(2)}) collective-permute-start(bf16[384,192]{0,1:T(8,128)(2,1)S(1)} %convolution_convert_fusion.13), channel_id=1, source_target_pairs={{0,4},{4,0},{8,12},{12,8},{16,20},{20,16},{24,28},{28,24},{1,5},{5... | collective-permute-start | bytes 442376 | tf_op jit(solution)/shard_map/ppermute | solution.py:24
  275.5 69.1 %collective-permute-start.59 = (bf16[384,1536]{1,0:T(8,128)(2,1)}, bf16[384,1536]{1,0:T(8,128)(2,1)}, u32[]{:S(2)}, u32[]{:S(2)}) collective-permute-start(bf16[384,1536]{1,0:T(8,128)(2,1)} %convolution_convert_fusion.3), channel_id=1, source_target_pairs={{0,4},{4,0},{8,12},{12,8},{16,20},{20,16},{24,28},{28,24},{1,5},{5... | collective-permute-start | bytes 3538952 | tf_op jit(solution)/shard_map/ppermute | solution.py:24
  276.0 15.0 %collective-permute-start.33 = (bf16[256,768]{1,0:T(8,128)(2,1)}, bf16[256,768]{1,0:T(8,128)(2,1)}, u32[]{:S(2)}, u32[]{:S(2)}) collective-permute-start(bf16[256,768]{1,0:T(8,128)(2,1)} %convolution_convert_fusion.7), channel_id=1, source_target_pairs={{0,3},{1,2},{2,1},{3,0},{4,7},{5,6},{6,5},{7,4},{8,11},{9,10},{10,... | collective-permute-start | bytes 1179656 | tf_op jit(solution)/shard_map/ppermute | solution.py:24
  277.5 33.2 %collective-permute-start.34 = (bf16[256,768]{1,0:T(8,128)(2,1)}, bf16[256,768]{1,0:T(8,128)(2,1)}, u32[]{:S(2)}, u32[]{:S(2)}) collective-permute-start(bf16[256,768]{1,0:T(8,128)(2,1)} %convolution_convert_fusion.6), channel_id=1, source_target_pairs={{0,2},{1,3},{2,0},{3,1},{4,6},{5,7},{6,4},{7,5},{8,10},{9,11},{10,... | collective-permute-start | bytes 1179656 | tf_op jit(solution)/shard_map/ppermute | solution.py:24
  277.5 33.2 %collective-permute-start.35 = (bf16[256,768]{1,0:T(8,128)(2,1)}, bf16[256,768]{1,0:T(8,128)(2,1)}, u32[]{:S(2)}, u32[]{:S(2)}) collective-permute-start(bf16[256,768]{1,0:T(8,128)(2,1)} %convolution_convert_fusion.5), channel_id=1, source_target_pairs={{0,1},{1,0},{2,3},{3,2},{4,5},{5,4},{6,7},{7,6},{8,9},{9,8},{10,11... | collective-permute-start | bytes 1179656 | tf_op jit(solution)/shard_map/ppermute | solution.py:24
  291.0 34.6 %collective-permute-start.43 = (bf16[384,576]{0,1:T(8,128)(2,1)}, bf16[384,576]{0,1:T(8,128)(2,1)}, u32[]{:S(2)}, u32[]{:S(2)}) collective-permute-start(bf16[384,576]{0,1:T(8,128)(2,1)} %convolution_convert_fusion.4), channel_id=1, source_target_pairs={{0,4},{4,0},{8,12},{12,8},{16,20},{20,16},{24,28},{28,24},{1,5},{5... | collective-permute-start | bytes 1327112 | tf_op jit(solution)/shard_map/ppermute | solution.py:24
  291.1 24.8 %collective-permute-start.48 = (bf16[96,192]{1,0:T(8,128)(2,1)S(1)}, bf16[96,192]{1,0:T(8,128)(2,1)S(1)}, u32[]{:S(2)}, u32[]{:S(2)}) collective-permute-start(bf16[96,192]{1,0:T(8,128)(2,1)S(1)} %fusion.109), channel_id=1, source_target_pairs={{0,16},{4,20},{8,24},{12,28},{16,0},{20,4},{24,8},{28,12},{1,17},{... | collective-permute-start | bytes 110600 | tf_op jit(solution)/shard_map/ppermute | solution.py:24
  323.3 23.0 %collective-permute-start.60 = (bf16[384,1536]{1,0:T(8,128)(2,1)}, bf16[384,1536]{1,0:T(8,128)(2,1)}, u32[]{:S(2)}, u32[]{:S(2)}) collective-permute-start(bf16[384,1536]{1,0:T(8,128)(2,1)} %convolution_convert_fusion.2), channel_id=1, source_target_pairs={{0,4},{4,0},{8,12},{12,8},{16,20},{20,16},{24,28},{28,24},{1,5},{5... | collective-permute-start | bytes 3538952 | tf_op jit(solution)/shard_map/ppermute | solution.py:24
  323.9 24.5 %collective-permute-start.61 = (bf16[384,1536]{1,0:T(8,128)(2,1)}, bf16[384,1536]{1,0:T(8,128)(2,1)}, u32[]{:S(2)}, u32[]{:S(2)}) collective-permute-start(bf16[384,1536]{1,0:T(8,128)(2,1)} %convolution_convert_fusion.1), channel_id=1, source_target_pairs={{0,4},{4,0},{8,12},{12,8},{16,20},{20,16},{24,28},{28,24},{1,5},{5... | collective-permute-start | bytes 3538952 | tf_op jit(solution)/shard_map/ppermute | solution.py:24
  324.0 8.2 %collective-permute-start.42 = (f32[1920]{0:T(1024)S(1)}, f32[1920]{0:T(1024)}, u32[]{:S(2)}, u32[]{:S(2)}) collective-permute-start(f32[1920]{0:T(1024)S(1)} %add_add_fusion.5), channel_id=1, source_target_pairs={{0,16},{4,20},{8,24},{12,28},{16,0},{20,4},{24,8},{28,12},{1,17},{... | collective-permute-start | bytes 23048 | tf_op jit(solution)/shard_map/ppermute | solution.py:24
  330.4 8.1 %collective-permute-start.44 = (bf16[192,576]{1,0:T(8,128)(2,1)S(1)}, bf16[192,576]{1,0:T(8,128)(2,1)S(1)}, u32[]{:S(2)}, u32[]{:S(2)}) collective-permute-start(bf16[192,576]{1,0:T(8,128)(2,1)S(1)} %bitcast.334), channel_id=1, source_target_pairs={{0,16},{4,20},{8,24},{12,28},{16,0},{20,4},{24,8},{28,12},{1,17},{... | collective-permute-start | bytes 663560 | tf_op jit(solution)/shard_map/ppermute | solution.py:24
  332.1 18.0 %collective-permute-start.62 = (bf16[384,1536]{1,0:T(8,128)(2,1)}, bf16[384,1536]{1,0:T(8,128)(2,1)}, u32[]{:S(2)}, u32[]{:S(2)}) collective-permute-start(bf16[384,1536]{1,0:T(8,128)(2,1)} %convolution_convert_fusion), channel_id=1, source_target_pairs={{0,4},{4,0},{8,12},{12,8},{16,20},{20,16},{24,28},{28,24},{1,5},{5... | collective-permute-start | bytes 3538952 | tf_op jit(solution)/shard_map/ppermute | solution.py:24
  352.5 16.3 %collective-permute-start.66 = (bf16[192,1536]{1,0:T(8,128)(2,1)S(1)}, bf16[192,1536]{1,0:T(8,128)(2,1)S(1)}, u32[]{:S(2)}, u32[]{:S(2)}) collective-permute-start(bf16[192,1536]{1,0:T(8,128)(2,1)S(1)} %bitcast.324), channel_id=1, source_target_pairs={{0,8},{4,12},{8,0},{12,4},{16,24},{20,28},{24,16},{28,20},{1,9},{5... | collective-permute-start | bytes 1769480 | tf_op jit(solution)/shard_map/ppermute | solution.py:24
  353.1 16.3 %collective-permute-start.65 = (bf16[192,1536]{1,0:T(8,128)(2,1)S(1)}, bf16[192,1536]{1,0:T(8,128)(2,1)S(1)}, u32[]{:S(2)}, u32[]{:S(2)}) collective-permute-start(bf16[192,1536]{1,0:T(8,128)(2,1)S(1)} %bitcast.325), channel_id=1, source_target_pairs={{0,16},{4,20},{8,24},{12,28},{16,0},{20,4},{24,8},{28,12},{1,17},{... | collective-permute-start | bytes 1769480 | tf_op jit(solution)/shard_map/ppermute | solution.py:24
  354.1 24.7 %collective-permute-start.63 = (bf16[192,1536]{1,0:T(8,128)(2,1)S(1)}, bf16[192,1536]{1,0:T(8,128)(2,1)S(1)}, u32[]{:S(2)}, u32[]{:S(2)}) collective-permute-start(bf16[192,1536]{1,0:T(8,128)(2,1)S(1)} %bitcast.326), channel_id=1, source_target_pairs={{0,16},{4,20},{8,24},{12,28},{16,0},{20,4},{24,8},{28,12},{1,17},{... | collective-permute-start | bytes 1769480 | tf_op jit(solution)/shard_map/ppermute | solution.py:24
  355.4 23.5 %collective-permute-start.64 = (bf16[192,1536]{1,0:T(8,128)(2,1)S(1)}, bf16[192,1536]{1,0:T(8,128)(2,1)S(1)}, u32[]{:S(2)}, u32[]{:S(2)}) collective-permute-start(bf16[192,1536]{1,0:T(8,128)(2,1)S(1)} %bitcast.323), channel_id=1, source_target_pairs={{0,8},{4,12},{8,0},{12,4},{16,24},{20,28},{24,16},{28,20},{1,9},{5... | collective-permute-start | bytes 1769480 | tf_op jit(solution)/shard_map/ppermute | solution.py:24
  379.2 9.2 %collective-permute-start.69 = (bf16[96,1536]{1,0:T(8,128)(2,1)S(1)}, bf16[96,1536]{1,0:T(8,128)(2,1)S(1)}, u32[]{:S(2)}, u32[]{:S(2)}) collective-permute-start(bf16[96,1536]{1,0:T(8,128)(2,1)S(1)} %fusion.58), channel_id=1, source_target_pairs={{0,8},{4,12},{8,0},{12,4},{16,24},{20,28},{24,16},{28,20},{1,9},{5... | collective-permute-start | bytes 884744 | tf_op jit(solution)/shard_map/ppermute | solution.py:24
  381.0 10.5 %collective-permute-start.67 = (bf16[96,1536]{1,0:T(8,128)(2,1)S(1)}, bf16[96,1536]{1,0:T(8,128)(2,1)S(1)}, u32[]{:S(2)}, u32[]{:S(2)}) collective-permute-start(bf16[96,1536]{1,0:T(8,128)(2,1)S(1)} %fusion.56), channel_id=1, source_target_pairs={{0,8},{4,12},{8,0},{12,4},{16,24},{20,28},{24,16},{28,20},{1,9},{5... | collective-permute-start | bytes 884744 | tf_op jit(solution)/shard_map/ppermute | solution.py:24
  381.4 10.2 %collective-permute-start.70 = (bf16[96,1536]{1,0:T(8,128)(2,1)S(1)}, bf16[96,1536]{1,0:T(8,128)(2,1)S(1)}, u32[]{:S(2)}, u32[]{:S(2)}) collective-permute-start(bf16[96,1536]{1,0:T(8,128)(2,1)S(1)} %fusion.59), channel_id=1, source_target_pairs={{0,16},{4,20},{8,24},{12,28},{16,0},{20,4},{24,8},{28,12},{1,17},{... | collective-permute-start | bytes 884744 | tf_op jit(solution)/shard_map/ppermute | solution.py:24
  382.2 10.9 %collective-permute-start.68 = (bf16[96,1536]{1,0:T(8,128)(2,1)S(1)}, bf16[96,1536]{1,0:T(8,128)(2,1)S(1)}, u32[]{:S(2)}, u32[]{:S(2)}) collective-permute-start(bf16[96,1536]{1,0:T(8,128)(2,1)S(1)} %fusion.57), channel_id=1, source_target_pairs={{0,16},{4,20},{8,24},{12,28},{16,0},{20,4},{24,8},{28,12},{1,17},{... | collective-permute-start | bytes 884744 | tf_op jit(solution)/shard_map/ppermute | solution.py:24
  393.3 23.2 %collective-permute-start.76 = (bf16[96,768]{1,0:T(8,128)(2,1)S(1)}, bf16[96,768]{1,0:T(8,128)(2,1)S(1)}, u32[]{:S(2)}, u32[]{:S(2)}) collective-permute-start(bf16[96,768]{1,0:T(8,128)(2,1)S(1)} %slice.421), channel_id=1, source_target_pairs={{0,1},{1,0},{2,3},{3,2},{4,5},{5,4},{6,7},{7,6},{8,9},{9,8},{10,11... | collective-permute-start | bytes 442376 | tf_op jit(solution)/shard_map/ppermute | solution.py:24
  394.4 8.9 %collective-permute-start.73 = (bf16[96,768]{1,0:T(8,128)(2,1)S(1)}, bf16[96,768]{1,0:T(8,128)(2,1)S(1)}, u32[]{:S(2)}, u32[]{:S(2)}) collective-permute-start(bf16[96,768]{1,0:T(8,128)(2,1)S(1)} %slice.422), channel_id=1, source_target_pairs={{0,1},{1,0},{2,3},{3,2},{4,5},{5,4},{6,7},{7,6},{8,9},{9,8},{10,11... | collective-permute-start | bytes 442376 | tf_op jit(solution)/shard_map/ppermute | solution.py:24
  395.4 11.9 %collective-permute-start.71 = (bf16[96,768]{1,0:T(8,128)(2,1)S(1)}, bf16[96,768]{1,0:T(8,128)(2,1)S(1)}, u32[]{:S(2)}, u32[]{:S(2)}) collective-permute-start(bf16[96,768]{1,0:T(8,128)(2,1)S(1)} %get-tuple-element.173), channel_id=1, source_target_pairs={{0,3},{1,2},{2,1},{3,0},{4,7},{5,6},{6,5},{7,4},{8,11},{9,10},{10,... | collective-permute-start | bytes 442376 | tf_op jit(solution)/shard_map/ppermute | solution.py:24
  397.2 18.5 %collective-permute-start.72 = (bf16[96,768]{1,0:T(8,128)(2,1)S(1)}, bf16[96,768]{1,0:T(8,128)(2,1)S(1)}, u32[]{:S(2)}, u32[]{:S(2)}) collective-permute-start(bf16[96,768]{1,0:T(8,128)(2,1)S(1)} %get-tuple-element.174), channel_id=1, source_target_pairs={{0,2},{1,3},{2,0},{3,1},{4,6},{5,7},{6,4},{7,5},{8,10},{9,11},{10,... | collective-permute-start | bytes 442376 | tf_op jit(solution)/shard_map/ppermute | solution.py:24
  397.9 18.6 %collective-permute-start.74 = (bf16[96,768]{1,0:T(8,128)(2,1)S(1)}, bf16[96,768]{1,0:T(8,128)(2,1)S(1)}, u32[]{:S(2)}, u32[]{:S(2)}) collective-permute-start(bf16[96,768]{1,0:T(8,128)(2,1)S(1)} %get-tuple-element.171), channel_id=1, source_target_pairs={{0,3},{1,2},{2,1},{3,0},{4,7},{5,6},{6,5},{7,4},{8,11},{9,10},{10,... | collective-permute-start | bytes 442376 | tf_op jit(solution)/shard_map/ppermute | solution.py:24
  403.3 15.8 %collective-permute-start.75 = (bf16[96,768]{1,0:T(8,128)(2,1)S(1)}, bf16[96,768]{1,0:T(8,128)(2,1)S(1)}, u32[]{:S(2)}, u32[]{:S(2)}) collective-permute-start(bf16[96,768]{1,0:T(8,128)(2,1)S(1)} %get-tuple-element.172), channel_id=1, source_target_pairs={{0,2},{1,3},{2,0},{3,1},{4,6},{5,7},{6,4},{7,5},{8,10},{9,11},{10,... | collective-permute-start | bytes 442376 | tf_op jit(solution)/shard_map/ppermute | solution.py:24
  (90 other events, 809.7 us)
where the time goes:
time: 424 us; the launch traced here: 420 us
  waiting for transfers between devices  170 us (40%)
  starting transfers between devices  100 us (24%)
  matrix products  64.9 us (15%)
  other arithmetic  50.8 us (12%)
  local copies, waits for them, and re-layouts  30.3 us (7%)
    ppermute x77, waiting for transfers between devices, swap(): return lax.ppermute(values, axis, [(i, i ^ mask) for i in range(count)])  170 us
    ppermute x77, starting transfers between devices, swap(): return lax.ppermute(values, axis, [(i, i ^ mask) for i in range(count)])  100 us
    dot_general x12, matrix products, dot_rows(): return lax.dot_general(left, right, ROWS_DIM, preferred_element_type=f32)  22.9 us
    concatenate x15, other arithmetic, gather_blocks(): held = jnp.concatenate([held, swap(held, axis, bit)], axis=0)  15.7 us
    dot_general x12, matrix products, dot_cols(): return lax.dot_general(left, right, COLS_DIM, preferred_element_type=f32)  12.4 us
    dot_general x12, matrix products, dot(): return jnp.dot(left, right, preferred_element_type=f32)  10.8 us
    unnamed x193, local copies, waits for them, and re-layouts  9.73 us
  transfers between devices with their start and end apart: 77, of which 33 were waited for; matrix products, arithmetic and copies ran while one was open for 23% of the time, Pallas kernels for 0%

commit v1 on v0

--- a/solution.py
+++ b/solution.py
@@ -119,15 +119,16 @@
     return values
 
 
-def after(values, *earlier):
-    return lax.optimization_barrier((values, *earlier))[0]
+def tie(values, *earlier):
+    zero = sum(jnp.minimum(jnp.abs(e[(0,) * e.ndim].astype(f32)), 0.0) for e in earlier)
+    return (values.astype(f32) + zero).astype(values.dtype)
 
 
 def join(chunks):
     return jnp.concatenate(chunks, axis=0)
 
 
-def attend_forward(queries, keys, values, segment, places, width, between):
+def attend_forward(queries, keys, values, segment, places, width):
     length, heads_here, head_size = queries.shape
     contexts, logsums = [], []
     for first in range(0, length, width):
@@ -144,13 +145,11 @@
         context = jnp.einsum("hqk,khe->qhe", weights, values, preferred_element_type=jnp.float32)
         contexts.append(context.astype(jnp.bfloat16).reshape(width, heads_here * head_size))
         logsums.append(largest + jnp.log(total))
-        if first == 0:
-            between(contexts[0])
     return join(contexts), logsums
 
 
 def attend_backward(
-    queries, keys, values, grad_context, logsums, segment, places, width, between
+    queries, keys, values, grad_context, logsums, segment, places, width
 ):
     length, heads_here, head_size = queries.shape
     grad_keys = jnp.zeros(keys.shape, jnp.float32)
@@ -181,8 +180,6 @@
             "hqk,qhe->khe", grad_scores, query_block, preferred_element_type=jnp.float32
         )
         grad_queries.append(grad_query.astype(jnp.bfloat16).reshape(width, heads_here * head_size))
-        if first == 0:
-            between(grad_queries[0])
     return (
         join(grad_queries),
         grad_keys.astype(jnp.bfloat16).reshape(length, heads_here * head_size),
@@ -263,31 +260,18 @@
     def halves(values):
         return values[..., :half], values[..., half:]
 
-    late_up, late_bias, late_down, queries, keys_all, values_all = lax.optimization_barrier(
-        (up_weight, up_bias, down_weight.T, queries, keys_all, values_all)
-    )
-    up_chunks = gather_chunks(late_up)
-    bias_parts = gather_chunks(late_bias)
-    stages = {}
-
-    def midway(block):
-        *up, arrived = lax.optimization_barrier((*up_chunks, block))
-        stages["up"] = [
+    up_chunks = gather_chunks(tie(up_weight, mixed[-1]))
+    down_chunks = gather_chunks(tie(down_weight.T, mixed[-1]))
+    bias_chunks = jnp.concatenate(gather_chunks(tie(up_bias, mixed[-1])))
+    whole_up, whole_down = (
+        [
             gather_blocks(part, "dp", order)
-            for part, order in zip(halves(jnp.concatenate(up, axis=1)), (order_a, order_b))
+            for part, order in zip(halves(jnp.concatenate(chunks, axis=1)), (order_a, order_b))
         ]
-        stages["down"] = gather_chunks(after(late_down, *up[1:], block))
-
-    context, logsum = attend_forward(
-        queries, keys_all, values_all, segment, places, width, midway
-    )
-    bias_chunks = jnp.concatenate(list(lax.optimization_barrier((*bias_parts, context)))[:-1])
-    whole_up = stages["up"]
-    down_chunks = lax.optimization_barrier((*stages["down"], context))[:-1]
-    whole_down = [
-        gather_blocks(part, "dp", order)
-        for part, order in zip(halves(jnp.concatenate(down_chunks, axis=1)), (order_a, order_b))
-    ]
+        for chunks in (up_chunks, down_chunks)
+    )
+    context, logsum = attend_forward(queries, keys_all, values_all, segment, places, width)
+    context = tie(context, *up_chunks[1:], *down_chunks[1:])
 
     grad_out = cotangent.astype(f32) * valid[:, None]
     grad_out_low = grad_out.astype(jnp.bfloat16)
@@ -327,17 +311,15 @@
             both,
         )
     ]
-    firsts, grad_context = lax.optimization_barrier((firsts, grad_context))
     sums = [meet(pair, "dp", order, 0) for pair, order in zip(firsts, both)]
     out_sum = scatter_product(join(chunks_hidden), context, "dp", order_b)
 
-    def step_sums(step, value):
-        sums[:] = lax.optimization_barrier((sums, value))[0]
-        if step < len(order_a):
-            sums[:] = [
-                meet(halve(total, "dp", order, step), "dp", order, step)
-                for total, order in zip(sums, both)
-            ]
+    grad_context = join([grad_context[:width], tie(grad_context[width:], *sums)])
+    for step in range(1, len(order_a)):
+        sums = [
+            meet(halve(total, "dp", order, step), "dp", order, step)
+            for total, order in zip(sums, both)
+        ]
 
     bias_sums = jnp.concatenate([jnp.sum(part, axis=0, dtype=f32) for part in grad_upper])
     bias_sums = bias_sums.reshape(group, hidden_units // group)
@@ -365,14 +347,10 @@
         segment,
         places,
         width,
-        lambda block: step_sums(1, block),
     )
     grad_queries = grad_queries * factor
     grad_mixed = jnp.concatenate([grad_queries, grad_keys, grad_values], axis=1)
-    for step in range(2, len(order_a)):
-        step_sums(step, grad_mixed)
     grad_normed_one = scatter_chunks(lambda r: dot_cols(rows_of(grad_mixed, r), whole_qkv))
-    step_sums(len(order_a), grad_normed_one)
     size = hidden_units // group
 
     def own_shard(parts):
@@ -388,7 +366,8 @@
     first_value, first_pull = jax.vjp(layer_norm, start_values, first_gain, first_shift)
     grad_start_norm, grad_first_gain, grad_first_shift = first_pull(grad_normed_one)
     grad_inputs = (grad_hidden + grad_start_norm).astype(jnp.bfloat16)
-    late = sum_over(jnp.concatenate([grad_first_gain, grad_first_shift]), "mp")
+    late = tie(jnp.concatenate([grad_first_gain, grad_first_shift]), *sums)
+    late = sum_over(late, "mp")
     late = sum_over(jnp.concatenate([late, grad_qv_bias]), "dp")
     return (
         result,

time: 424 us -> 401 us (0.946)
  waiting for transfers between devices: 170 us -> 128 us
  local copies, waits for them, and re-layouts: 30.3 us -> 57.7 us
  starting transfers between devices: 100 us -> 88.9 us
  between operations: 4 us -> 13.8 us
  other arithmetic: 50.8 us -> 44.8 us
    ppermute x77, waiting for transfers between devices: 170 us -> 128 us  [swap(): return lax.ppermute(values, axis, [(i, i ^ mask) for i in range(count)])]
    ppermute x77, starting transfers between devices: 100 us -> 88.9 us  [swap(): return lax.ppermute(values, axis, [(i, i ^ mask) for i in range(count)])]
    dynamic_slice x8, local copies, waits for them, and re-layouts: 0.85 us -> 11.2 us  [halve(): lax.dynamic_index_in_dim(total, half, place, keepdims=False)]
    slice x4 -> x16, local copies, waits for them, and re-layouts: 0.63 us -> 7.74 us  [the longest x15 7.74 us: tie(): e[(0,) * e.ndim].astype(f32)]
    unnamed x193 -> x217, local copies, waits for them, and re-layouts: 9.73 us -> 12.4 us
  transfers between devices with their start and end apart: 77 -> 77, of which waited for: 33 -> 27; matrix products, arithmetic and copies ran while one was open for 23% -> 31% of each run, Pallas kernels for 0% -> 0%
where the time goes in v1:
time: 401 us; the launch traced here: 397 us
  waiting for transfers between devices  128 us (32%)
  starting transfers between devices  88.9 us (22%)
  matrix products  63.8 us (16%)
  local copies, waits for them, and re-layouts  57.7 us (14%)
  other arithmetic  44.8 us (11%)
  between operations  13.8 us (3%)
    ppermute x77, waiting for transfers between devices, swap(): return lax.ppermute(values, axis, [(i, i ^ mask) for i in range(count)])  128 us
    ppermute x77, starting transfers between devices, swap(): return lax.ppermute(values, axis, [(i, i ^ mask) for i in range(count)])  88.9 us
    dot_general x12, matrix products, dot_rows(): return lax.dot_general(left, right, ROWS_DIM, preferred_element_type=f32)  18.6 us
    concatenate x15, other arithmetic, gather_blocks(): held = jnp.concatenate([held, swap(held, axis, bit)], axis=0)  14 us
    dot_general x12, matrix products, dot(): return jnp.dot(left, right, preferred_element_type=f32)  12.5 us
    unnamed x217, local copies, waits for them, and re-layouts  12.4 us
    dot_general x12, matrix products, dot_cols(): return lax.dot_general(left, right, COLS_DIM, preferred_element_type=f32)  12.1 us
    dynamic_slice x8, local copies, waits for them, and re-layouts, halve(): lax.dynamic_index_in_dim(total, half, place, keepdims=False)  11.2 us
  transfers between devices with their start and end apart: 77, of which 27 were waited for; matrix products, arithmetic and copies ran while one was open for 31% of the time, Pallas kernels for 0%

profile of v1, /device:TPU:0, one launch (start us, length us, event | category | flops | bytes accessed | tf_op | source)
XLA Modules:
  0.0 396.6 jit_solution(9243556584027673000)
XLA Ops:
  4.4 5.1 %collective-permute-start.5 = (bf16[256,768]{1,0:T(8,128)(2,1)S(1)}, bf16[256,768]{1,0:T(8,128)(2,1)}, u32[]{:S(2)}, u32[]{:S(2)}) collective-permute-start(bf16[256,768]{1,0:T(8,128)(2,1)S(1)} %fusion.49), channel_id=1, source_target_pairs={{0,3},{1,2},{2,1},{3,0},{4,7},{5,6},{6,5},{7,4},{8,11},{9,10},{10,... | collective-permute-start | bytes 1179656 | tf_op jit(solution)/shard_map/ppermute | solution.py:24
  12.1 1.7 collective-permute-start
  19.9 7.9 %collective-permute-done.1 = bf16[2,96,768]{1,2,0:T(8,128)(2,1)S(1)} collective-permute-done((bf16[2,96,768]{1,2,0:T(8,128)(2,1)S(1)}, bf16[2,96,768]{1,2,0:T(8,128)(2,1)S(1)}, u32[]{:S(2)}, u32[]{:S(2)}) %collective-permute-start.1) | collective-permute-done | bytes 294944 | tf_op jit(solution)/shard_map/ppermute | solution.py:24
  30.6 12.5 %collective-permute-done.4 = bf16[256,768]{1,0:T(8,128)(2,1)S(1)} collective-permute-done((bf16[256,768]{1,0:T(8,128)(2,1)S(1)}, bf16[256,768]{1,0:T(8,128)(2,1)S(1)}, u32[]{:S(2)}, u32[]{:S(2)}) %collective-permute-start.4) | collective-permute-done | bytes 393248 | tf_op jit(solution)/shard_map/ppermute | solution.py:24
  43.1 2.4 pad_maximum_fusion.4
  45.5 2.6 copy.203
  48.0 2.6 constant_dynamic-slice_fusion.6
  55.0 2.5 collective-permute-start.26
  57.5 1.9 collective-permute-start.18
  59.5 2.5 collective-permute-start.8
  68.8 2.0 fusion.44
  74.8 2.5 fusion.45
  77.3 2.0 collective-permute-start.6
  79.3 2.5 collective-permute-start.11
  81.8 1.9 collective-permute-start.9
  87.2 2.3 collective-permute-done.11
  90.7 1.9 collective-permute-done.10
  101.4 2.0 collective-permute-start.12
  103.3 3.7 collective-permute-done.22
  107.1 2.8 collective-permute-start.14
  116.7 15.3 %collective-permute-done.13 = bf16[256,768]{1,0:T(8,128)(2,1)S(1)} collective-permute-done((bf16[256,768]{1,0:T(8,128)(2,1)S(1)}, bf16[256,768]{1,0:T(8,128)(2,1)S(1)}, u32[]{:S(2)}, u32[]{:S(2)}) %collective-permute-start.13) | collective-permute-done | bytes 393248 | tf_op jit(solution)/shard_map/ppermute | solution.py:24
  135.4 8.8 %collective-permute-done.23 = bf16[2,96,1536]{2,1,0:T(8,128)(2,1)S(1)} collective-permute-done((bf16[2,96,1536]{2,1,0:T(8,128)(2,1)S(1)}, bf16[2,96,1536]{2,1,0:T(8,128)(2,1)S(1)}, u32[]{:S(2)}, u32[]{:S(2)}) %collective-permute-start.23) | collective-permute-done | bytes 589856 | tf_op jit(solution)/shard_map/ppermute | solution.py:24
  146.4 1.9 copy.201
  148.4 1.8 constant_dynamic-slice_fusion.13
  174.6 2.3 collective-permute-start.65
  176.9 2.9 collective-permute-start.66
  183.0 2.0 collective-permute-start.61
  190.6 2.7 collective-permute-start.30
  195.4 1.7 collective-permute-done.70
  197.7 12.8 %collective-permute-done.30 = bf16[256,768]{1,0:T(8,128)(2,1)S(1)} collective-permute-done((bf16[256,768]{1,0:T(8,128)(2,1)S(1)}, bf16[256,768]{1,0:T(8,128)(2,1)S(1)}, u32[]{:S(2)}, u32[]{:S(2)}) %collective-permute-start.30) | collective-permute-done | bytes 393248 | tf_op jit(solution)/shard_map/ppermute | solution.py:24
  211.1 2.4 multiply_reduce_fusion.1
  213.6 1.7 multiply_convert_fusion.1
  215.3 1.8 convolution_convert_fusion.12
  221.9 2.8 copy.206
  229.4 2.1 reshape.525
  231.5 1.9 constant_dynamic-slice_fusion
  233.3 1.7 copy.212
  236.5 1.8 constant_dynamic-slice_fusion.1
  238.3 1.7 copy.207
  242.8 2.2 convolution_convert_fusion.15
  247.7 2.1 convert_add_fusion.1
  251.0 1.8 convert_add_fusion.3
  254.9 1.9 convert_add_fusion
  263.1 1.8 convert_add_fusion.2
  266.2 1.7 fusion.4
  268.0 2.4 multiply_reduce_fusion
  270.4 1.9 convert_reduce_fusion.3
  272.3 2.0 multiply_convert_fusion
  284.0 2.4 collective-permute-start.37
  289.6 2.4 constant_dynamic-slice_fusion.9
  291.9 6.3 %collective-permute-done.37 = bf16[256,768]{1,0:T(8,128)(2,1)S(1)} collective-permute-done((bf16[256,768]{1,0:T(8,128)(2,1)}, bf16[256,768]{1,0:T(8,128)(2,1)S(1)}, u32[]{:S(2)}, u32[]{:S(2)}) %collective-permute-start.37) | collective-permute-done | bytes 393248 | tf_op jit(solution)/shard_map/ppermute | solution.py:24
  299.7 21.2 %collective-permute-done.38 = bf16[256,768]{1,0:T(8,128)(2,1)S(1)} collective-permute-done((bf16[256,768]{1,0:T(8,128)(2,1)}, bf16[256,768]{1,0:T(8,128)(2,1)S(1)}, u32[]{:S(2)}, u32[]{:S(2)}) %collective-permute-start.38) | collective-permute-done | bytes 393248 | tf_op jit(solution)/shard_map/ppermute | solution.py:24
  322.7 2.1 fusion.52
  326.5 1.8 convert_add_fusion.5
  341.9 2.5 collective-permute-done.45
  345.6 5.1 %collective-permute-done.41 = bf16[96,1536]{1,0:T(8,128)(2,1)S(1)} collective-permute-done((bf16[96,1536]{1,0:T(8,128)(2,1)S(1)}, bf16[96,1536]{1,0:T(8,128)(2,1)S(1)}, u32[]{:S(2)}, u32[]{:S(2)}) %collective-permute-start.41) | collective-permute-done | bytes 294944 | tf_op jit(solution)/shard_map/ppermute | solution.py:24
  354.5 2.4 collective-permute-start.50
  356.9 3.2 collective-permute-start.49
  361.2 2.1 collective-permute-start.76
  367.1 2.4 collective-permute-start.74
  371.2 2.6 collective-permute-done.54
  373.8 2.3 collective-permute-start.71
  377.9 12.1 %collective-permute-done.75 = bf16[96,768]{1,0:T(8,128)(2,1)S(1)} collective-permute-done((bf16[96,768]{1,0:T(8,128)(2,1)S(1)}, bf16[96,768]{1,0:T(8,128)(2,1)S(1)}, u32[]{:S(2)}, u32[]{:S(2)}) %collective-permute-start.75) | collective-permute-done | bytes 147488 | tf_op jit(solution)/shard_map/ppermute | solution.py:24
  390.8 4.7 %collective-permute-done.72 = bf16[96,768]{1,0:T(8,128)(2,1)S(1)} collective-permute-done((bf16[96,768]{1,0:T(8,128)(2,1)S(1)}, bf16[96,768]{1,0:T(8,128)(2,1)S(1)}, u32[]{:S(2)}, u32[]{:S(2)}) %collective-permute-start.72) | collective-permute-done | bytes 147488 | tf_op jit(solution)/shard_map/ppermute | solution.py:24
  (526 shorter events, 154.3 us)
Async XLA Ops:
  4.4 26.2 %collective-permute-start.5 = (bf16[256,768]{1,0:T(8,128)(2,1)S(1)}, bf16[256,768]{1,0:T(8,128)(2,1)}, u32[]{:S(2)}, u32[]{:S(2)}) collective-permute-start(bf16[256,768]{1,0:T(8,128)(2,1)S(1)} %fusion.49), channel_id=1, source_target_pairs={{0,3},{1,2},{2,1},{3,0},{4,7},{5,6},{6,5},{7,4},{8,11},{9,10},{10,... | collective-permute-start | bytes 1179656 | tf_op jit(solution)/shard_map/ppermute | solution.py:24
  9.5 33.5 %collective-permute-start.4 = (bf16[256,768]{1,0:T(8,128)(2,1)S(1)}, bf16[256,768]{1,0:T(8,128)(2,1)S(1)}, u32[]{:S(2)}, u32[]{:S(2)}) collective-permute-start(bf16[256,768]{1,0:T(8,128)(2,1)S(1)} %fusion.49), channel_id=1, source_target_pairs={{0,2},{1,3},{2,0},{3,1},{4,6},{5,7},{6,4},{7,5},{8,10},{9,11},{10,... | collective-permute-start | bytes 1179656 | tf_op jit(solution)/shard_map/ppermute | solution.py:24
  9.5 33.5 %collective-permute-start.3 = (bf16[256,768]{1,0:T(8,128)(2,1)S(1)}, bf16[256,768]{1,0:T(8,128)(2,1)}, u32[]{:S(2)}, u32[]{:S(2)}) collective-permute-start(bf16[256,768]{1,0:T(8,128)(2,1)S(1)} %fusion.49), channel_id=1, source_target_pairs={{0,1},{1,0},{2,3},{3,2},{4,5},{5,4},{6,7},{7,6},{8,9},{9,8},{10,11... | collective-permute-start | bytes 1179656 | tf_op jit(solution)/shard_map/ppermute | solution.py:24
  12.1 6.1 %collective-permute-start = (bf16[1,96,768]{1,2,0:T(8,128)(2,1)S(1)}, bf16[1,96,768]{1,2,0:T(8,128)(2,1)S(1)}, u32[]{:S(2)}, u32[]{:S(2)}) collective-permute-start(bf16[1,96,768]{1,2,0:T(8,128)(2,1)S(1)} %maximum_bitcast_fusion.4), channel_id=1, source_target_pairs={{0,8},{4,12},{8,0},{12,4},{16,24},{20,28},{24,16},{28,20},{1,9},{5... | collective-permute-start | bytes 442376 | tf_op jit(solution)/shard_map/ppermute | solution.py:24
  18.3 9.5 %collective-permute-start.1 = (bf16[2,96,768]{1,2,0:T(8,128)(2,1)S(1)}, bf16[2,96,768]{1,2,0:T(8,128)(2,1)S(1)}, u32[]{:S(2)}, u32[]{:S(2)}) collective-permute-start(bf16[2,96,768]{1,2,0:T(8,128)(2,1)S(1)} %pad_maximum_fusion.17), channel_id=1, source_target_pairs={{0,16},{4,20},{8,24},{12,28},{16,0},{20,4},{24,8},{28,12},{1,17},{... | collective-permute-start | bytes 884744 | tf_op jit(solution)/shard_map/ppermute | solution.py:24
  29.1 21.7 %collective-permute-start.2 = (bf16[4,96,768]{2,1,0:T(8,128)(2,1)}, bf16[4,96,768]{2,1,0:T(8,128)(2,1)}, u32[]{:S(2)}, u32[]{:S(2)}) collective-permute-start(bf16[4,96,768]{2,1,0:T(8,128)(2,1)} %copy.196), channel_id=1, source_target_pairs={{0,4},{4,0},{8,12},{12,8},{16,20},{20,16},{24,28},{28,24},{1,5},{5... | collective-permute-start | bytes 1769480 | tf_op jit(solution)/shard_map/ppermute | solution.py:24
  55.0 22.3 %collective-permute-start.26 = (f32[768]{0:T(1024)S(1)}, f32[768]{0:T(1024)S(1)}, u32[]{:S(2)}, u32[]{:S(2)}) collective-permute-start(f32[768]{0:T(1024)S(1)} %broadcast_add_fusion), channel_id=1, source_target_pairs={{0,3},{1,2},{2,1},{3,0},{4,7},{5,6},{6,5},{7,4},{8,11},{9,10},{10,... | collective-permute-start | bytes 9224 | tf_op jit(solution)/shard_map/ppermute | solution.py:24
  57.5 21.8 %collective-permute-start.25 = (f32[768]{0:T(1024)S(1)}, f32[768]{0:T(1024)S(1)}, u32[]{:S(2)}, u32[]{:S(2)}) collective-permute-start(f32[768]{0:T(1024)S(1)} %broadcast_add_fusion), channel_id=1, source_target_pairs={{0,2},{1,3},{2,0},{3,1},{4,6},{5,7},{6,4},{7,5},{8,10},{9,11},{10,... | collective-permute-start | bytes 9224 | tf_op jit(solution)/shard_map/ppermute | solution.py:24
  57.5 24.2 %collective-permute-start.18 = (f32[768]{0:T(1024)S(1)}, f32[768]{0:T(1024)S(1)}, u32[]{:S(2)}, u32[]{:S(2)}) collective-permute-start(f32[768]{0:T(1024)S(1)} %broadcast_add_fusion), channel_id=1, source_target_pairs={{0,1},{1,0},{2,3},{3,2},{4,5},{5,4},{6,7},{7,6},{8,9},{9,8},{10,11... | collective-permute-start | bytes 9224 | tf_op jit(solution)/shard_map/ppermute | solution.py:24
  59.5 22.3 %collective-permute-start.8 = (bf16[96,768]{1,0:T(8,128)(2,1)S(1)}, bf16[96,768]{1,0:T(8,128)(2,1)S(1)}, u32[]{:S(2)}, u32[]{:S(2)}) collective-permute-start(bf16[96,768]{1,0:T(8,128)(2,1)S(1)} %add_convert_fusion.5), channel_id=1, source_target_pairs={{0,3},{1,2},{2,1},{3,0},{4,7},{5,6},{6,5},{7,4},{8,11},{9,10},{10,... | collective-permute-start | bytes 442376 | tf_op jit(solution)/shard_map/ppermute | solution.py:24
  62.0 22.8 %collective-permute-start.7 = (bf16[96,768]{1,0:T(8,128)(2,1)S(1)}, bf16[96,768]{1,0:T(8,128)(2,1)S(1)}, u32[]{:S(2)}, u32[]{:S(2)}) collective-permute-start(bf16[96,768]{1,0:T(8,128)(2,1)S(1)} %add_convert_fusion.5), channel_id=1, source_target_pairs={{0,2},{1,3},{2,0},{3,1},{4,6},{5,7},{6,4},{7,5},{8,10},{9,11},{10,... | collective-permute-start | bytes 442376 | tf_op jit(solution)/shard_map/ppermute | solution.py:24
  77.3 8.7 %collective-permute-start.6 = (bf16[96,768]{1,0:T(8,128)(2,1)S(1)}, bf16[96,768]{1,0:T(8,128)(2,1)S(1)}, u32[]{:S(2)}, u32[]{:S(2)}) collective-permute-start(bf16[96,768]{1,0:T(8,128)(2,1)S(1)} %add_convert_fusion.5), channel_id=1, source_target_pairs={{0,1},{1,0},{2,3},{3,2},{4,5},{5,4},{6,7},{7,6},{8,9},{9,8},{10,11... | collective-permute-start | bytes 442376 | tf_op jit(solution)/shard_map/ppermute | solution.py:24
  79.3 10.2 %collective-permute-start.11 = (bf16[96,768]{1,0:T(8,128)(2,1)S(1)}, bf16[96,768]{1,0:T(8,128)(2,1)S(1)}, u32[]{:S(2)}, u32[]{:S(2)}) collective-permute-start(bf16[96,768]{1,0:T(8,128)(2,1)S(1)} %fusion.96), channel_id=1, source_target_pairs={{0,3},{1,2},{2,1},{3,0},{4,7},{5,6},{6,5},{7,4},{8,11},{9,10},{10,... | collective-permute-start | bytes 442376 | tf_op jit(solution)/shard_map/ppermute | solution.py:24
  81.8 10.8 %collective-permute-start.10 = (bf16[96,768]{1,0:T(8,128)(2,1)S(1)}, bf16[96,768]{1,0:T(8,128)(2,1)S(1)}, u32[]{:S(2)}, u32[]{:S(2)}) collective-permute-start(bf16[96,768]{1,0:T(8,128)(2,1)S(1)} %fusion.96), channel_id=1, source_target_pairs={{0,2},{1,3},{2,0},{3,1},{4,6},{5,7},{6,4},{7,5},{8,10},{9,11},{10,... | collective-permute-start | bytes 442376 | tf_op jit(solution)/shard_map/ppermute | solution.py:24
  81.8 12.0 %collective-permute-start.9 = (bf16[96,768]{1,0:T(8,128)(2,1)S(1)}, bf16[96,768]{1,0:T(8,128)(2,1)S(1)}, u32[]{:S(2)}, u32[]{:S(2)}) collective-permute-start(bf16[96,768]{1,0:T(8,128)(2,1)S(1)} %fusion.96), channel_id=1, source_target_pairs={{0,1},{1,0},{2,3},{3,2},{4,5},{5,4},{6,7},{7,6},{8,9},{9,8},{10,11... | collective-permute-start | bytes 442376 | tf_op jit(solution)/shard_map/ppermute | solution.py:24
  96.9 10.2 %collective-permute-start.19 = (bf16[1,96,1536]{2,1,0:T(8,128)(2,1)S(1)}, bf16[1,96,1536]{2,1,0:T(8,128)(2,1)S(1)}, u32[]{:S(2)}, u32[]{:S(2)}) collective-permute-start(bf16[1,96,1536]{2,1,0:T(8,128)(2,1)S(1)} %maximum_bitcast_fusion.1), channel_id=1, source_target_pairs={{0,8},{4,12},{8,0},{12,4},{16,24},{20,28},{24,16},{28,20},{1,9},{5... | collective-permute-start | bytes 884744 | tf_op jit(solution)/shard_map/ppermute | solution.py:24
  98.5 8.5 %collective-permute-start.22 = (bf16[1,96,1536]{2,1,0:T(8,128)(2,1)S(1)}, bf16[1,96,1536]{2,1,0:T(8,128)(2,1)S(1)}, u32[]{:S(2)}, u32[]{:S(2)}) collective-permute-start(bf16[1,96,1536]{2,1,0:T(8,128)(2,1)S(1)} %maximum_bitcast_fusion.2), channel_id=1, source_target_pairs={{0,16},{4,20},{8,24},{12,28},{16,0},{20,4},{24,8},{28,12},{1,17},{... | collective-permute-start | bytes 884744 | tf_op jit(solution)/shard_map/ppermute | solution.py:24
  100.1 11.7 %collective-permute-start.27 = (bf16[1,96,1536]{2,1,0:T(8,128)(2,1)S(1)}, bf16[1,96,1536]{2,1,0:T(8,128)(2,1)S(1)}, u32[]{:S(2)}, u32[]{:S(2)}) collective-permute-start(bf16[1,96,1536]{2,1,0:T(8,128)(2,1)S(1)} %maximum_bitcast_fusion.3), channel_id=1, source_target_pairs={{0,16},{4,20},{8,24},{12,28},{16,0},{20,4},{24,8},{28,12},{1,17},{... | collective-permute-start | bytes 884744 | tf_op jit(solution)/shard_map/ppermute | solution.py:24
  100.8 12.7 %collective-permute-start.15 = (bf16[1,96,1536]{2,1,0:T(8,128)(2,1)S(1)}, bf16[1,96,1536]{2,1,0:T(8,128)(2,1)S(1)}, u32[]{:S(2)}, u32[]{:S(2)}) collective-permute-start(bf16[1,96,1536]{2,1,0:T(8,128)(2,1)S(1)} %maximum_bitcast_fusion), channel_id=1, source_target_pairs={{0,8},{4,12},{8,0},{12,4},{16,24},{20,28},{24,16},{28,20},{1,9},{5... | collective-permute-start | bytes 884744 | tf_op jit(solution)/shard_map/ppermute | solution.py:24
  101.4 13.9 %collective-permute-start.12 = (bf16[256,768]{1,0:T(8,128)(2,1)S(1)}, bf16[256,768]{1,0:T(8,128)(2,1)S(1)}, u32[]{:S(2)}, u32[]{:S(2)}) collective-permute-start(bf16[256,768]{1,0:T(8,128)(2,1)S(1)} %convolution_convert_fusion.10), channel_id=1, source_target_pairs={{0,3},{1,2},{2,1},{3,0},{4,7},{5,6},{6,5},{7,4},{8,11},{9,10},{10,... | collective-permute-start | bytes 1179656 | tf_op jit(solution)/shard_map/ppermute | solution.py:24
  107.0 25.0 %collective-permute-start.13 = (bf16[256,768]{1,0:T(8,128)(2,1)S(1)}, bf16[256,768]{1,0:T(8,128)(2,1)S(1)}, u32[]{:S(2)}, u32[]{:S(2)}) collective-permute-start(bf16[256,768]{1,0:T(8,128)(2,1)S(1)} %convolution_convert_fusion.9), channel_id=1, source_target_pairs={{0,2},{1,3},{2,0},{3,1},{4,6},{5,7},{6,4},{7,5},{8,10},{9,11},{10,... | collective-permute-start | bytes 1179656 | tf_op jit(solution)/shard_map/ppermute | solution.py:24
  107.1 26.4 %collective-permute-start.14 = (bf16[256,768]{1,0:T(8,128)(2,1)S(1)}, bf16[256,768]{1,0:T(8,128)(2,1)S(1)}, u32[]{:S(2)}, u32[]{:S(2)}) collective-permute-start(bf16[256,768]{1,0:T(8,128)(2,1)S(1)} %convolution_convert_fusion.8), channel_id=1, source_target_pairs={{0,1},{1,0},{2,3},{3,2},{4,5},{5,4},{6,7},{7,6},{8,9},{9,8},{10,11... | collective-permute-start | bytes 1179656 | tf_op jit(solution)/shard_map/ppermute | solution.py:24
  111.9 38.3 %collective-permute-start.20 = (bf16[2,96,1536]{2,1,0:T(8,128)(2,1)}, bf16[2,96,1536]{2,1,0:T(8,128)(2,1)}, u32[]{:S(2)}, u32[]{:S(2)}) collective-permute-start(bf16[2,96,1536]{2,1,0:T(8,128)(2,1)} %pad_maximum_fusion.14), channel_id=1, source_target_pairs={{0,16},{4,20},{8,24},{12,28},{16,0},{20,4},{24,8},{28,12},{1,17},{... | collective-permute-start | bytes 1769480 | tf_op jit(solution)/shard_map/ppermute | solution.py:24
  113.5 20.7 %collective-permute-start.28 = (bf16[2,96,1536]{2,1,0:T(8,128)(2,1)S(1)}, bf16[2,96,1536]{2,1,0:T(8,128)(2,1)S(1)}, u32[]{:S(2)}, u32[]{:S(2)}) collective-permute-start(bf16[2,96,1536]{2,1,0:T(8,128)(2,1)S(1)} %pad_maximum_fusion.16), channel_id=1, source_target_pairs={{0,8},{4,12},{8,0},{12,4},{16,24},{20,28},{24,16},{28,20},{1,9},{5... | collective-permute-start | bytes 1769480 | tf_op jit(solution)/shard_map/ppermute | solution.py:24
  115.2 37.0 %collective-permute-start.16 = (bf16[2,96,1536]{2,1,0:T(8,128)(2,1)}, bf16[2,96,1536]{2,1,0:T(8,128)(2,1)}, u32[]{:S(2)}, u32[]{:S(2)}) collective-permute-start(bf16[2,96,1536]{2,1,0:T(8,128)(2,1)} %pad_maximum_fusion.13), channel_id=1, source_target_pairs={{0,16},{4,20},{8,24},{12,28},{16,0},{20,4},{24,8},{28,12},{1,17},{... | collective-permute-start | bytes 1769480 | tf_op jit(solution)/shard_map/ppermute | solution.py:24
  132.0 12.2 %collective-permute-start.23 = (bf16[2,96,1536]{2,1,0:T(8,128)(2,1)S(1)}, bf16[2,96,1536]{2,1,0:T(8,128)(2,1)S(1)}, u32[]{:S(2)}, u32[]{:S(2)}) collective-permute-start(bf16[2,96,1536]{2,1,0:T(8,128)(2,1)S(1)} %pad_maximum_fusion.15), channel_id=1, source_target_pairs={{0,8},{4,12},{8,0},{12,4},{16,24},{20,28},{24,16},{28,20},{1,9},{5... | collective-permute-start | bytes 1769480 | tf_op jit(solution)/shard_map/ppermute | solution.py:24
  135.4 18.1 %collective-permute-start.29 = (bf16[4,96,1536]{2,1,0:T(8,128)(2,1)}, bf16[4,96,1536]{2,1,0:T(8,128)(2,1)}, u32[]{:S(2)}, u32[]{:S(2)}) collective-permute-start(bf16[4,96,1536]{2,1,0:T(8,128)(2,1)} %pad_maximum_fusion.10), channel_id=1, source_target_pairs={{0,4},{4,0},{8,12},{12,8},{16,20},{20,16},{24,28},{28,24},{1,5},{5... | collective-permute-start | bytes 3538952 | tf_op jit(solution)/shard_map/ppermute | solution.py:24
  145.5 9.7 %collective-permute-start.24 = (bf16[4,96,1536]{2,1,0:T(8,128)(2,1)}, bf16[4,96,1536]{2,1,0:T(8,128)(2,1)}, u32[]{:S(2)}, u32[]{:S(2)}) collective-permute-start(bf16[4,96,1536]{2,1,0:T(8,128)(2,1)} %pad_maximum_fusion.9), channel_id=1, source_target_pairs={{0,4},{4,0},{8,12},{12,8},{16,20},{20,16},{24,28},{28,24},{1,5},{5... | collective-permute-start | bytes 3538952 | tf_op jit(solution)/shard_map/ppermute | solution.py:24
  151.6 5.6 %collective-permute-start.21 = (bf16[4,96,1536]{2,1,0:T(8,128)(2,1)S(1)}, bf16[4,96,1536]{2,1,0:T(8,128)(2,1)S(1)}, u32[]{:S(2)}, u32[]{:S(2)}) collective-permute-start(bf16[4,96,1536]{2,1,0:T(8,128)(2,1)S(1)} %pad_maximum_fusion.8), channel_id=1, source_target_pairs={{0,4},{4,0},{8,12},{12,8},{16,20},{20,16},{24,28},{28,24},{1,5},{5... | collective-permute-start | bytes 3538952 | tf_op jit(solution)/shard_map/ppermute | solution.py:24
  153.4 5.9 %collective-permute-start.17 = (bf16[4,96,1536]{2,1,0:T(8,128)(2,1)S(1)}, bf16[4,96,1536]{2,1,0:T(8,128)(2,1)S(1)}, u32[]{:S(2)}, u32[]{:S(2)}) collective-permute-start(bf16[4,96,1536]{2,1,0:T(8,128)(2,1)S(1)} %pad_maximum_fusion.7), channel_id=1, source_target_pairs={{0,4},{4,0},{8,12},{12,8},{16,20},{20,16},{24,28},{28,24},{1,5},{5... | collective-permute-start | bytes 3538952 | tf_op jit(solution)/shard_map/ppermute | solution.py:24
  170.0 16.6 %collective-permute-start.62 = (f32[3072]{0:T(1024)S(1)}, f32[3072]{0:T(1024)S(1)}, u32[]{:S(2)}, u32[]{:S(2)}) collective-permute-start(f32[3072]{0:T(1024)S(1)} %pad_maximum_fusion.24), channel_id=1, source_target_pairs={{0,2},{1,3},{2,0},{3,1},{4,6},{5,7},{6,4},{7,5},{8,10},{9,11},{10,... | collective-permute-start | bytes 36872 | tf_op jit(solution)/shard_map/ppermute | solution.py:24
  170.1 16.5 %collective-permute-start.63 = (f32[3072]{0:T(1024)S(1)}, f32[3072]{0:T(1024)S(1)}, u32[]{:S(2)}, u32[]{:S(2)}) collective-permute-start(f32[3072]{0:T(1024)S(1)} %pad_maximum_fusion.24), channel_id=1, source_target_pairs={{0,3},{1,2},{2,1},{3,0},{4,7},{5,6},{6,5},{7,4},{8,11},{9,10},{10,... | collective-permute-start | bytes 36872 | tf_op jit(solution)/shard_map/ppermute | solution.py:24
  174.6 8.4 %collective-permute-start.65 = (f32[768]{0:T(1024)S(1)}, f32[768]{0:T(1024)S(1)}, u32[]{:S(2)}, u32[]{:S(2)}) collective-permute-start(f32[768]{0:T(1024)S(1)} %get-tuple-element.132), channel_id=1, source_target_pairs={{0,2},{1,3},{2,0},{3,1},{4,6},{5,7},{6,4},{7,5},{8,10},{9,11},{10,... | collective-permute-start | bytes 9224 | tf_op jit(solution)/shard_map/ppermute | solution.py:24
  176.9 8.1 %collective-permute-start.66 = (f32[768]{0:T(1024)S(1)}, f32[768]{0:T(1024)S(1)}, u32[]{:S(2)}, u32[]{:S(2)}) collective-permute-start(f32[768]{0:T(1024)S(1)} %get-tuple-element.133), channel_id=1, source_target_pairs={{0,3},{1,2},{2,1},{3,0},{4,7},{5,6},{6,5},{7,4},{8,11},{9,10},{10,... | collective-permute-start | bytes 9224 | tf_op jit(solution)/shard_map/ppermute | solution.py:24
  179.9 6.1 %collective-permute-start.64 = (f32[768]{0:T(1024)S(1)}, f32[768]{0:T(1024)S(1)}, u32[]{:S(2)}, u32[]{:S(2)}) collective-permute-start(f32[768]{0:T(1024)S(1)} %slice.372), channel_id=1, source_target_pairs={{0,1},{1,0},{2,3},{3,2},{4,5},{5,4},{6,7},{7,6},{8,9},{9,8},{10,11... | collective-permute-start | bytes 9224 | tf_op jit(solution)/shard_map/ppermute | solution.py:24
  185.0 33.6 %collective-permute-start.32 = (bf16[256,768]{1,0:T(8,128)(2,1)S(1)}, bf16[256,768]{1,0:T(8,128)(2,1)S(1)}, u32[]{:S(2)}, u32[]{:S(2)}) collective-permute-start(bf16[256,768]{1,0:T(8,128)(2,1)S(1)} %get-tuple-element.110), channel_id=1, source_target_pairs={{0,3},{1,2},{2,1},{3,0},{4,7},{5,6},{6,5},{7,4},{8,11},{9,10},{10,... | collective-permute-start | bytes 1179656 | tf_op jit(solution)/shard_map/ppermute | solution.py:24
  185.9 33.9 %collective-permute-start.31 = (bf16[256,768]{1,0:T(8,128)(2,1)S(1)}, bf16[256,768]{1,0:T(8,128)(2,1)S(1)}, u32[]{:S(2)}, u32[]{:S(2)}) collective-permute-start(bf16[256,768]{1,0:T(8,128)(2,1)S(1)} %get-tuple-element.110), channel_id=1, source_target_pairs={{0,2},{1,3},{2,0},{3,1},{4,6},{5,7},{6,4},{7,5},{8,10},{9,11},{10,... | collective-permute-start | bytes 1179656 | tf_op jit(solution)/shard_map/ppermute | solution.py:24
  190.6 20.0 %collective-permute-start.30 = (bf16[256,768]{1,0:T(8,128)(2,1)S(1)}, bf16[256,768]{1,0:T(8,128)(2,1)S(1)}, u32[]{:S(2)}, u32[]{:S(2)}) collective-permute-start(bf16[256,768]{1,0:T(8,128)(2,1)S(1)} %get-tuple-element.110), channel_id=1, source_target_pairs={{0,1},{1,0},{2,3},{3,2},{4,5},{5,4},{6,7},{7,6},{8,9},{9,8},{10,11... | collective-permute-start | bytes 1179656 | tf_op jit(solution)/shard_map/ppermute | solution.py:24
  193.3 54.4 %collective-permute-start.35 = (bf16[384,1536]{1,0:T(8,128)(2,1)}, bf16[384,1536]{1,0:T(8,128)(2,1)}, u32[]{:S(2)}, u32[]{:S(2)}) collective-permute-start(bf16[384,1536]{1,0:T(8,128)(2,1)} %convolution_convert_fusion.1), channel_id=1, source_target_pairs={{0,4},{4,0},{8,12},{12,8},{16,20},{20,16},{24,28},{28,24},{1,5},{5... | collective-permute-start | bytes 3538952 | tf_op jit(solution)/shard_map/ppermute | solution.py:24
  197.1 53.9 %collective-permute-start.33 = (bf16[384,1536]{1,0:T(8,128)(2,1)}, bf16[384,1536]{1,0:T(8,128)(2,1)}, u32[]{:S(2)}, u32[]{:S(2)}) collective-permute-start(bf16[384,1536]{1,0:T(8,128)(2,1)} %convolution_convert_fusion.3), channel_id=1, source_target_pairs={{0,4},{4,0},{8,12},{12,8},{16,20},{20,16},{24,28},{28,24},{1,5},{5... | collective-permute-start | bytes 3538952 | tf_op jit(solution)/shard_map/ppermute | solution.py:24
  210.5 44.4 %collective-permute-start.36 = (bf16[384,1536]{1,0:T(8,128)(2,1)}, bf16[384,1536]{1,0:T(8,128)(2,1)}, u32[]{:S(2)}, u32[]{:S(2)}) collective-permute-start(bf16[384,1536]{1,0:T(8,128)(2,1)} %convolution_convert_fusion), channel_id=1, source_target_pairs={{0,4},{4,0},{8,12},{12,8},{16,20},{20,16},{24,28},{28,24},{1,5},{5... | collective-permute-start | bytes 3538952 | tf_op jit(solution)/shard_map/ppermute | solution.py:24
  218.6 44.5 %collective-permute-start.34 = (bf16[384,1536]{1,0:T(8,128)(2,1)}, bf16[384,1536]{1,0:T(8,128)(2,1)}, u32[]{:S(2)}, u32[]{:S(2)}) collective-permute-start(bf16[384,1536]{1,0:T(8,128)(2,1)} %convolution_convert_fusion.2), channel_id=1, source_target_pairs={{0,4},{4,0},{8,12},{12,8},{16,20},{20,16},{24,28},{28,24},{1,5},{5... | collective-permute-start | bytes 3538952 | tf_op jit(solution)/shard_map/ppermute | solution.py:24
  280.4 50.7 %collective-permute-start.44 = (bf16[192,1536]{1,0:T(8,128)(2,1)}, bf16[192,1536]{1,0:T(8,128)(2,1)}, u32[]{:S(2)}, u32[]{:S(2)}) collective-permute-start(bf16[192,1536]{1,0:T(8,128)(2,1)} %bitcast.95), channel_id=1, source_target_pairs={{0,16},{4,20},{8,24},{12,28},{16,0},{20,4},{24,8},{28,12},{1,17},{... | collective-permute-start | bytes 1769480 | tf_op jit(solution)/shard_map/ppermute | solution.py:24
  281.9 51.6 %collective-permute-start.40 = (bf16[192,1536]{1,0:T(8,128)(2,1)}, bf16[192,1536]{1,0:T(8,128)(2,1)}, u32[]{:S(2)}, u32[]{:S(2)}) collective-permute-start(bf16[192,1536]{1,0:T(8,128)(2,1)} %bitcast.83), channel_id=1, source_target_pairs={{0,16},{4,20},{8,24},{12,28},{16,0},{20,4},{24,8},{28,12},{1,17},{... | collective-permute-start | bytes 1769480 | tf_op jit(solution)/shard_map/ppermute | solution.py:24
  284.0 14.2 %collective-permute-start.37 = (bf16[256,768]{1,0:T(8,128)(2,1)}, bf16[256,768]{1,0:T(8,128)(2,1)S(1)}, u32[]{:S(2)}, u32[]{:S(2)}) collective-permute-start(bf16[256,768]{1,0:T(8,128)(2,1)} %convolution_convert_fusion.7), channel_id=1, source_target_pairs={{0,3},{1,2},{2,1},{3,0},{4,7},{5,6},{6,5},{7,4},{8,11},{9,10},{10,... | collective-permute-start | bytes 1179656 | tf_op jit(solution)/shard_map/ppermute | solution.py:24
  286.4 34.4 %collective-permute-start.38 = (bf16[256,768]{1,0:T(8,128)(2,1)}, bf16[256,768]{1,0:T(8,128)(2,1)S(1)}, u32[]{:S(2)}, u32[]{:S(2)}) collective-permute-start(bf16[256,768]{1,0:T(8,128)(2,1)} %convolution_convert_fusion.6), channel_id=1, source_target_pairs={{0,2},{1,3},{2,0},{3,1},{4,6},{5,7},{6,4},{7,5},{8,10},{9,11},{10,... | collective-permute-start | bytes 1179656 | tf_op jit(solution)/shard_map/ppermute | solution.py:24
  287.8 34.9 %collective-permute-start.39 = (bf16[256,768]{1,0:T(8,128)(2,1)}, bf16[256,768]{1,0:T(8,128)(2,1)}, u32[]{:S(2)}, u32[]{:S(2)}) collective-permute-start(bf16[256,768]{1,0:T(8,128)(2,1)} %convolution_convert_fusion.5), channel_id=1, source_target_pairs={{0,1},{1,0},{2,3},{3,2},{4,5},{5,4},{6,7},{7,6},{8,9},{9,8},{10,11... | collective-permute-start | bytes 1179656 | tf_op jit(solution)/shard_map/ppermute | solution.py:24
  298.2 37.8 %collective-permute-start.46 = (bf16[192,1536]{1,0:T(8,128)(2,1)}, bf16[192,1536]{1,0:T(8,128)(2,1)}, u32[]{:S(2)}, u32[]{:S(2)}) collective-permute-start(bf16[192,1536]{1,0:T(8,128)(2,1)} %bitcast.101), channel_id=1, source_target_pairs={{0,8},{4,12},{8,0},{12,4},{16,24},{20,28},{24,16},{28,20},{1,9},{5... | collective-permute-start | bytes 1769480 | tf_op jit(solution)/shard_map/ppermute | solution.py:24
  321.6 16.7 %collective-permute-start.42 = (bf16[192,1536]{1,0:T(8,128)(2,1)}, bf16[192,1536]{1,0:T(8,128)(2,1)}, u32[]{:S(2)}, u32[]{:S(2)}) collective-permute-start(bf16[192,1536]{1,0:T(8,128)(2,1)} %bitcast.89), channel_id=1, source_target_pairs={{0,8},{4,12},{8,0},{12,4},{16,24},{20,28},{24,16},{28,20},{1,9},{5... | collective-permute-start | bytes 1769480 | tf_op jit(solution)/shard_map/ppermute | solution.py:24
  330.0 10.8 %collective-permute-start.56 = (bf16[192,576]{1,0:T(8,128)(2,1)S(1)}, bf16[192,576]{1,0:T(8,128)(2,1)S(1)}, u32[]{:S(2)}, u32[]{:S(2)}) collective-permute-start(bf16[192,576]{1,0:T(8,128)(2,1)S(1)} %bitcast.344), channel_id=1, source_target_pairs={{0,16},{4,20},{8,24},{12,28},{16,0},{20,4},{24,8},{28,12},{1,17},{... | collective-permute-start | bytes 663560 | tf_op jit(solution)/shard_map/ppermute | solution.py:24
  332.5 11.9 %collective-permute-start.45 = (bf16[96,1536]{1,0:T(8,128)(2,1)S(1)}, bf16[96,1536]{1,0:T(8,128)(2,1)S(1)}, u32[]{:S(2)}, u32[]{:S(2)}) collective-permute-start(bf16[96,1536]{1,0:T(8,128)(2,1)S(1)} %fusion.58), channel_id=1, source_target_pairs={{0,8},{4,12},{8,0},{12,4},{16,24},{20,28},{24,16},{28,20},{1,9},{5... | collective-permute-start | bytes 884744 | tf_op jit(solution)/shard_map/ppermute | solution.py:24
  334.8 15.8 %collective-permute-start.41 = (bf16[96,1536]{1,0:T(8,128)(2,1)S(1)}, bf16[96,1536]{1,0:T(8,128)(2,1)S(1)}, u32[]{:S(2)}, u32[]{:S(2)}) collective-permute-start(bf16[96,1536]{1,0:T(8,128)(2,1)S(1)} %fusion.56), channel_id=1, source_target_pairs={{0,8},{4,12},{8,0},{12,4},{16,24},{20,28},{24,16},{28,20},{1,9},{5... | collective-permute-start | bytes 884744 | tf_op jit(solution)/shard_map/ppermute | solution.py:24
  337.3 14.6 %collective-permute-start.47 = (bf16[96,1536]{1,0:T(8,128)(2,1)S(1)}, bf16[96,1536]{1,0:T(8,128)(2,1)S(1)}, u32[]{:S(2)}, u32[]{:S(2)}) collective-permute-start(bf16[96,1536]{1,0:T(8,128)(2,1)S(1)} %fusion.59), channel_id=1, source_target_pairs={{0,16},{4,20},{8,24},{12,28},{16,0},{20,4},{24,8},{28,12},{1,17},{... | collective-permute-start | bytes 884744 | tf_op jit(solution)/shard_map/ppermute | solution.py:24
  339.7 13.5 %collective-permute-start.43 = (bf16[96,1536]{1,0:T(8,128)(2,1)S(1)}, bf16[96,1536]{1,0:T(8,128)(2,1)S(1)}, u32[]{:S(2)}, u32[]{:S(2)}) collective-permute-start(bf16[96,1536]{1,0:T(8,128)(2,1)S(1)} %fusion.57), channel_id=1, source_target_pairs={{0,16},{4,20},{8,24},{12,28},{16,0},{20,4},{24,8},{28,12},{1,17},{... | collective-permute-start | bytes 884744 | tf_op jit(solution)/shard_map/ppermute | solution.py:24
  340.9 19.2 %collective-permute-start.57 = (bf16[96,576]{1,0:T(8,128)(2,1)S(1)}, bf16[96,576]{1,0:T(8,128)(2,1)S(1)}, u32[]{:S(2)}, u32[]{:S(2)}) collective-permute-start(bf16[96,576]{1,0:T(8,128)(2,1)S(1)} %fusion.97), channel_id=1, source_target_pairs={{0,8},{4,12},{8,0},{12,4},{16,24},{20,28},{24,16},{28,20},{1,9},{5... | collective-permute-start | bytes 331784 | tf_op jit(solution)/shard_map/ppermute | solution.py:24
  354.5 8.9 %collective-permute-start.50 = (f32[1536]{0:T(1024)S(1)}, f32[1536]{0:T(1024)S(1)}, u32[]{:S(2)}, u32[]{:S(2)}) collective-permute-start(f32[1536]{0:T(1024)S(1)} %maximum_add_fusion), channel_id=1, source_target_pairs={{0,3},{1,2},{2,1},{3,0},{4,7},{5,6},{6,5},{7,4},{8,11},{9,10},{10,... | collective-permute-start | bytes 18440 | tf_op jit(solution)/shard_map/ppermute | solution.py:24
  356.9 6.5 %collective-permute-start.49 = (f32[1536]{0:T(1024)S(1)}, f32[1536]{0:T(1024)S(1)}, u32[]{:S(2)}, u32[]{:S(2)}) collective-permute-start(f32[1536]{0:T(1024)S(1)} %maximum_add_fusion), channel_id=1, source_target_pairs={{0,2},{1,3},{2,0},{3,1},{4,6},{5,7},{6,4},{7,5},{8,10},{9,11},{10,... | collective-permute-start | bytes 18440 | tf_op jit(solution)/shard_map/ppermute | solution.py:24
  361.2 16.1 %collective-permute-start.76 = (bf16[96,768]{1,0:T(8,128)(2,1)S(1)}, bf16[96,768]{1,0:T(8,128)(2,1)S(1)}, u32[]{:S(2)}, u32[]{:S(2)}) collective-permute-start(bf16[96,768]{1,0:T(8,128)(2,1)S(1)} %slice.493), channel_id=1, source_target_pairs={{0,1},{1,0},{2,3},{3,2},{4,5},{5,4},{6,7},{7,6},{8,9},{9,8},{10,11... | collective-permute-start | bytes 442376 | tf_op jit(solution)/shard_map/ppermute | solution.py:24
  363.3 27.5 %collective-permute-start.73 = (bf16[96,768]{1,0:T(8,128)(2,1)S(1)}, bf16[96,768]{1,0:T(8,128)(2,1)S(1)}, u32[]{:S(2)}, u32[]{:S(2)}) collective-permute-start(bf16[96,768]{1,0:T(8,128)(2,1)S(1)} %slice.494), channel_id=1, source_target_pairs={{0,1},{1,0},{2,3},{3,2},{4,5},{5,4},{6,7},{7,6},{8,9},{9,8},{10,11... | collective-permute-start | bytes 442376 | tf_op jit(solution)/shard_map/ppermute | solution.py:24
  364.0 5.4 %collective-permute-start.52 = (f32[1920]{0:T(1024)S(1)}, f32[1920]{0:T(1024)S(1)}, u32[]{:S(2)}, u32[]{:S(2)}) collective-permute-start(f32[1920]{0:T(1024)S(1)} %concatenate.199), channel_id=1, source_target_pairs={{0,8},{4,12},{8,0},{12,4},{16,24},{20,28},{24,16},{28,20},{1,9},{5... | collective-permute-start | bytes 23048 | tf_op jit(solution)/shard_map/ppermute | solution.py:24
  367.1 10.9 %collective-permute-start.74 = (bf16[96,768]{1,0:T(8,128)(2,1)S(1)}, bf16[96,768]{1,0:T(8,128)(2,1)S(1)}, u32[]{:S(2)}, u32[]{:S(2)}) collective-permute-start(bf16[96,768]{1,0:T(8,128)(2,1)S(1)} %get-tuple-element.123), channel_id=1, source_target_pairs={{0,3},{1,2},{2,1},{3,0},{4,7},{5,6},{6,5},{7,4},{8,11},{9,10},{10,... | collective-permute-start | bytes 442376 | tf_op jit(solution)/shard_map/ppermute | solution.py:24
  369.4 20.6 %collective-permute-start.75 = (bf16[96,768]{1,0:T(8,128)(2,1)S(1)}, bf16[96,768]{1,0:T(8,128)(2,1)S(1)}, u32[]{:S(2)}, u32[]{:S(2)}) collective-permute-start(bf16[96,768]{1,0:T(8,128)(2,1)S(1)} %get-tuple-element.124), channel_id=1, source_target_pairs={{0,2},{1,3},{2,0},{3,1},{4,6},{5,7},{6,4},{7,5},{8,10},{9,11},{10,... | collective-permute-start | bytes 442376 | tf_op jit(solution)/shard_map/ppermute | solution.py:24
  373.8 17.0 %collective-permute-start.71 = (bf16[96,768]{1,0:T(8,128)(2,1)S(1)}, bf16[96,768]{1,0:T(8,128)(2,1)S(1)}, u32[]{:S(2)}, u32[]{:S(2)}) collective-permute-start(bf16[96,768]{1,0:T(8,128)(2,1)S(1)} %get-tuple-element.125), channel_id=1, source_target_pairs={{0,3},{1,2},{2,1},{3,0},{4,7},{5,6},{6,5},{7,4},{8,11},{9,10},{10,... | collective-permute-start | bytes 442376 | tf_op jit(solution)/shard_map/ppermute | solution.py:24
  377.3 18.2 %collective-permute-start.72 = (bf16[96,768]{1,0:T(8,128)(2,1)S(1)}, bf16[96,768]{1,0:T(8,128)(2,1)S(1)}, u32[]{:S(2)}, u32[]{:S(2)}) collective-permute-start(bf16[96,768]{1,0:T(8,128)(2,1)S(1)} %get-tuple-element.126), channel_id=1, source_target_pairs={{0,2},{1,3},{2,0},{3,1},{4,6},{5,7},{6,4},{7,5},{8,10},{9,11},{10,... | collective-permute-start | bytes 442376 | tf_op jit(solution)/shard_map/ppermute | solution.py:24
  (103 other events, 900.5 us)
